TPU v7x, 1024 devices: a whole 4x4x32 slice. The times are simulated.
1024 devices in a mesh: dp: 16 (over x, y), fsdp: 16 (over z_lo, core), seq: 4 (over z_hi).
Axes of the slice: x: 4, y: 4, z: 32 (z_hi: 4, z_lo: 8; z = z_hi * 8 + z_lo), core: 2. Of those that a mesh axis runs over, the one named last changes fastest.
Arguments:
- tokens: bfloat16 [256, 2048, 3200], P(('dp', 'fsdp'), 'seq'), may hold values from -300 to 300
- query: bfloat16 [16, 200], replicated, may hold values from -4 to 4
- value_weight: bfloat16 [3200, 768], P('fsdp'), may hold values from -0.109375 to 0.109375
- frames: int32 [256], P(('dp', 'fsdp')), may hold values from 4 to 16
- text_feat: float32 [256, 768], P(('dp', 'fsdp')), may hold values from -6 to 6
- pair: int32 [256], replicated, may hold values from 0 to 255, each once
- logit_scale: float32 [], replicated, may hold values from 10 to 60
Outputs:
- video_embed: float32 [256, 768], P(('dp', 'fsdp'))
- grad_video: float32 [256, 768], P(('dp', 'fsdp'))
- grad_text: float32 [256, 768], P(('dp', 'fsdp'))
- loss: float32 [], replicated
All inputs are finite; a program needn't handle non-finite values.
Results may differ from a plain program's by a relative error of at most 0.0003.
Values may be sent and summed in bfloat16 or wider, within the bound.
No kernel may reach another device: no remote copies, remote signals or barrier semaphores. Data moves between devices by JAX's collectives and lax.ppermute only.
A program may use at most 32 MiB of HBM per device.

v0:
```python
import jax
import jax.numpy as jnp
from jax import lax
from jax.sharding import PartitionSpec as P

FT = 128


def merged(value, axis, join):
    pieces = jax.tree.map(lambda part: lax.all_gather(part, axis), value)
    head = jax.tree.map(lambda part: part[0], pieces)
    tail = jax.tree.map(lambda part: part[1:], pieces)
    so_far, _ = lax.scan(lambda so_far, section: (join(so_far, section), None), head, tail)
    return so_far


def combine_states(first, second):
    top = jnp.maximum(first[0], second[0])
    left = jnp.exp(first[0] - top)
    right = jnp.exp(second[0] - top)
    total = first[1] * left + second[1] * right
    accum = first[2] * left[:, None] + second[2] * right[:, None]
    return (top, total, accum)


def unit_rows(values):
    return values * lax.rsqrt(jnp.sum(values * values, axis=1, keepdims=True) + 1e-06)


def shards(tokens, query, value_weight, frames, text_feat, pair, logit_scale):
    local_tok = tokens[0]
    rows = local_tok.shape[0]
    heads = query.shape[0]
    slice_w = query.shape[1]
    embed_w = value_weight.shape[1]
    position = lax.axis_index("seq") * rows + jnp.arange(rows, dtype=jnp.int32)
    valid = position // FT < frames[0]
    scores = jnp.einsum(
        "thd,hd->th",
        local_tok.reshape(rows, heads, slice_w),
        query,
        preferred_element_type=jnp.float32,
    ) / jnp.sqrt(jnp.float32(slice_w))
    scores = jnp.where(valid[:, None], scores, jnp.float32(-1e30))
    local_top = jnp.max(scores, axis=0)
    expd = jnp.where(valid[:, None], jnp.exp(scores - local_top[None, :]), jnp.float32(0.0))
    local_total = jnp.sum(expd, axis=0)
    values = jnp.dot(
        local_tok,
        lax.all_gather(value_weight, "fsdp", axis=0, tiled=True),
        preferred_element_type=jnp.float32,
    )
    accum = jnp.einsum(
        "th,the->he",
        expd,
        values.reshape(rows, heads, embed_w // heads),
        precision=lax.Precision.HIGHEST,
    )
    top, total, accum = merged((local_top, local_total, accum), "seq", combine_states)
    pooled = (accum / total[:, None]).reshape(1, embed_w)
    video_embed = unit_rows(pooled)
    text_unit = unit_rows(text_feat)
    videos_all, texts_all = (
        lax.all_gather(video_embed, ("dp", "fsdp"), axis=0, tiled=True),
        lax.all_gather(text_unit, ("dp", "fsdp"), axis=0, tiled=True),
    )
    count = videos_all.shape[0]
    logits = logit_scale * jnp.dot(videos_all, texts_all.T, precision=lax.Precision.HIGHEST)
    row_top = jnp.max(logits, axis=1)
    row_lse = row_top + jnp.log(jnp.sum(jnp.exp(logits - row_top[:, None]), axis=1))
    col_top = jnp.max(logits, axis=0)
    col_lse = col_top + jnp.log(jnp.sum(jnp.exp(logits - col_top[None, :]), axis=0))
    onehot = pair[:, None] == jnp.arange(count, dtype=jnp.int32)[None, :]
    positive = jnp.sum(jnp.where(onehot, logits, jnp.float32(0.0)), axis=1)
    loss = (jnp.sum(row_lse) + jnp.sum(col_lse) - 2.0 * jnp.sum(positive)) / (2.0 * count)
    grad_logits = (
        jnp.exp(logits - row_lse[:, None])
        + jnp.exp(logits - col_lse[None, :])
        - 2.0 * onehot.astype(jnp.float32)
    ) / (2.0 * count)
    own = lax.axis_index(("dp", "fsdp"))
    row_grad = lax.dynamic_slice_in_dim(grad_logits, own, 1, 0)
    col_grad = lax.dynamic_slice_in_dim(grad_logits, own, 1, 1).T
    grad_video = logit_scale * jnp.dot(row_grad, texts_all, precision=lax.Precision.HIGHEST)
    grad_text = logit_scale * jnp.dot(col_grad, videos_all, precision=lax.Precision.HIGHEST)
    return (video_embed, grad_video, grad_text, loss)


def solution(mesh):
    return jax.shard_map(
        shards,
        mesh=mesh,
        in_specs=(
            P(("dp", "fsdp"), "seq", None),
            P(),
            P("fsdp", None),
            P(("dp", "fsdp")),
            P(("dp", "fsdp"), None),
            P(),
            P(),
        ),
        out_specs=(P(("dp", "fsdp"), None), P(("dp", "fsdp"), None), P(("dp", "fsdp"), None), P()),
        check_vma=False,
    )
```

profile of v0, /device:TPU:1, one launch (start us, length us, event | category | flops | bytes accessed | tf_op | source)
XLA Modules:
  0.0 1153.5 jit_solution(14736200234167025454)
XLA Ops:
  7.2 0.7 all-gather.7.cloned.1.call-update
  9.2 1.3 multiply_reduce_fusion.1
  11.2 4.0 copy.15
  15.3 1.3 dynamic-slice
  17.2 0.6 fusion.22
  17.9 0.2 dynamic-update-slice
  18.4 0.2 dynamic-update-slice.1
  18.6 35.1 %all-reduce.2 = (f32[64]{0:T(128)S(1)}, f32[64]{0:T(128)S(1)}) all-reduce(f32[64]{0:T(128)S(1)} %dynamic-update-slice, f32[64]{0:T(128)S(1)} %dynamic-update-slice.1), channel_id=2, replica_groups=mesh['dp'=16,'fsdp'=16,'seq'=4] {'seq'}, use_global_device_ids=true, to_apply=%add | all-reduce | flops 128 | bytes 1024
  54.0 526.2 %all-gather.4 = f32[256,1,768]{2,1,0:T(1,128)S(1)} all-gather(f32[1,1,768]{2,1,0:T(1,128)S(1)} %multiply_bitcast_fusion), channel_id=1, replica_groups=mesh['dp'=16,'fsdp'=16,'seq'=4] {'dp','fsdp'}, dimensions={0}, use_global_device_ids=true | all-gather | bytes 789504 | tf_op jit(solution)/shard_map/all_gather | solution.py:65
  580.3 7.4 copy.16
  587.7 5.8 fusion.6
  593.5 1.4 fusion.17
  594.9 24.0 %all-gather.2 = f32[64,48]{1,0:T(8,128)S(1)} all-gather(f32[16,48]{1,0:T(8,128)S(1)} %bitcast.82), channel_id=4, replica_groups=mesh['dp'=16,'fsdp'=16,'seq'=4] {'seq'}, dimensions={0}, use_global_device_ids=true | all-gather | bytes 15360 | tf_op jit(solution)/shard_map/all_gather | solution.py:10
  618.9 0.3 while.14
  619.2 0.7 multiply_reduce_fusion
  620.8 0.7 mul.99
  621.4 517.3 %all-gather.3 = f32[256,1,768]{2,1,0:T(1,128)S(1)} all-gather(f32[1,1,768]{2,1,0:T(1,128)S(1)} %reshape.114), channel_id=1, replica_groups=mesh['dp'=16,'fsdp'=16,'seq'=4] {'dp','fsdp'}, dimensions={0}, use_global_device_ids=true | all-gather | bytes 789504 | tf_op jit(solution)/shard_map/all_gather | solution.py:64
  1138.7 0.9 fusion.31
  1139.6 0.8 select_reduce_fusion
  1140.4 0.7 fusion.33
  1141.3 0.5 convolution_reduce_fusion.1
  1141.9 0.5 convolution_reduce_fusion
  1142.5 0.6 mul.112
  1143.1 0.6 mul.110
  (32 shorter events, 1.5 us)
Async XLA Ops:
  7.2 573.1 %all-gather.7.cloned.1.call-start = ((), (), s32[]{:S(2)}) async-start(), calls=%async_computation | async-start | bytes 5222400 | tf_op jit(solution)/shard_map/all_gather | solution.py:50
  11.2 6.0 copy-start
  15.2 38.8 %copy-start.1 = (f32[1,768]{1,0:T(1,128)S(1)}, f32[1,768]{1,0:T(1,128)}, u32[]{:S(2)}) copy-start(f32[1,768]{1,0:T(1,128)} %param.13) | copy-start | bytes 9220
  593.5 546.2 %copy-start.2 = (s32[256]{0:T(256)S(1)}, s32[256]{0:T(256)}, u32[]{:S(2)}) copy-start(s32[256]{0:T(256)} %param.14) | copy-start | bytes 3076
Sparse Core Ops, SparseCore 0:
  10.7 125.2 all-gather.6
where the time goes:
time: 1150 us
  blocking collectives  1100 us (96%)
  between operations  20.5 us (2%)
  local copies, waits for them, and re-layouts  15.6 us (1%)
    all_gather x1, blocking collectives, shards(): lax.all_gather(text_unit, ('dp', 'fsdp'), axis=0, tiled=True)  526 us
    all_gather x1, blocking collectives, shards(): lax.all_gather(video_embed, ('dp', 'fsdp'), axis=0, tiled=True)  517 us
    unnamed x1, blocking collectives  35.1 us
    all_gather x1, blocking collectives, merged(): pieces = jax.tree.map(lambda part: lax.all_gather(part, axis), value)  24 us
  transfers between devices with their start and end apart: 1, of which 0 were waited for; matrix products, arithmetic and copies ran while one was open for 1% of the time, Pallas kernels for 0%

commit v1 on v0

v1 whole, which is shorter than its diff:
```python
import jax
import jax.numpy as jnp
from jax import lax
from jax.experimental import pallas as pl
from jax.experimental.pallas import tpu as pltpu
from jax.sharding import Mesh, PartitionSpec as P

D, E, H, FT = 3200, 768, 16, 128
W_H = D // H
W_E = E // H
CHUNKS = 16
ROWS = D // CHUNKS
TOK = 512
FRAMES_HERE = TOK // FT
HIGH = lax.Precision.HIGHEST
F32, BF16 = jnp.float32, jnp.bfloat16
VMEM_LIMIT = 40 * 1024 * 1024


def three_terms(value):
    first = value.astype(BF16)
    rest = value - first.astype(F32)
    second = rest.astype(BF16)
    third = (rest - second.astype(F32)).astype(BF16)
    return first, second, third


def pool_kernel(frames_ref, query_ref, tok_hbm, parts_ref, state_ref, tok, spread, mixed, sems):
    copies = [
        pltpu.make_async_copy(tok_hbm.at[0, pl.ds(FT * j, FT)], tok.at[pl.ds(FT * j, FT)], sems.at[j])
        for j in range(FRAMES_HERE)
    ]
    for copy in copies:
        copy.start()
    spread[...] = jnp.zeros_like(spread)
    rows = query_ref[...].astype(F32)
    for h in range(H):
        spread[h : h + 1, W_H * h : W_H * (h + 1)] = rows[h : h + 1, :]
    heads_q = spread[...].astype(BF16)
    used = frames_ref[0] - lax.axis_index("s") * FRAMES_HERE
    scores = []
    for j in range(FRAMES_HERE):
        copies[j].wait()
        part = lax.dot_general(
            heads_q, tok[FT * j : FT * (j + 1), :], (((1,), (1,)), ((), ())), preferred_element_type=F32
        )
        scores.append(jnp.where(j < used, part * F32(W_H**-0.5), F32(-1e30)))
    score = jnp.concatenate(scores, axis=1)
    top = jnp.max(score, axis=1, keepdims=True)
    frame = lax.broadcasted_iota(jnp.int32, (H, TOK), 1) // FT
    expd = jnp.where(frame < used, jnp.exp(score - top), F32(0.0))
    total = jnp.sum(expd, axis=1, keepdims=True)
    terms = jnp.concatenate(three_terms(expd), axis=0)
    step = 640
    for n in range(D // step):
        cols = slice(step * n, step * (n + 1))
        out = jnp.dot(terms, tok[:, cols], preferred_element_type=F32)
        mixed[:, cols] = (out[2 * H :] + out[H : 2 * H]) + out[:H]
    for k in range(CHUNKS):
        parts_ref[k, :, 0:ROWS] = mixed[:, ROWS * k : ROWS * (k + 1)]
    lane = lax.broadcasted_iota(jnp.int32, (H, 128), 1)
    head = lax.broadcasted_iota(jnp.int32, (H, 128), 0)
    row = jnp.where(lane == 64 + head, top, 0.0) + jnp.where(lane == 80 + head, total, 0.0)
    state_ref[...] = jnp.broadcast_to(jnp.sum(row, axis=0, keepdims=True), (8, 128))


def pool(frames, query, tokens):
    return pl.pallas_call(
        pool_kernel,
        out_shape=(
            jax.ShapeDtypeStruct((CHUNKS, H, 256), F32),
            jax.ShapeDtypeStruct((8, 128), F32),
        ),
        in_specs=[
            pl.BlockSpec(memory_space=pltpu.SMEM),
            pl.BlockSpec(memory_space=pltpu.VMEM),
            pl.BlockSpec(memory_space=pl.ANY),
        ],
        out_specs=(pl.BlockSpec(memory_space=pltpu.VMEM), pl.BlockSpec(memory_space=pltpu.VMEM)),
        scratch_shapes=[
            pltpu.VMEM((TOK, D), BF16),
            pltpu.VMEM((H, D), F32),
            pltpu.VMEM((H, D), F32),
            pltpu.SemaphoreType.DMA((FRAMES_HERE,)),
        ],
        compiler_params=pltpu.CompilerParams(vmem_limit_bytes=VMEM_LIMIT),
        cost_estimate=pl.CostEstimate(flops=4 * 64 * TOK * D, bytes_accessed=TOK * D * 2, transcendentals=H * TOK),
        name="pool",
    )(frames, query, tokens)


def project_kernel(parts_ref, weight_ref, out_ref):
    x = parts_ref[...].reshape(CHUNKS * H, 256)[:, :ROWS]
    first, second, third = three_terms(x)
    weight = weight_ref[...]
    own = lax.broadcasted_iota(jnp.int32, (H, 256), 0)
    lane = lax.broadcasted_iota(jnp.int32, (H, 256), 1)
    for n in range(E // 256):
        w = weight[:, 256 * n : 256 * (n + 1)]
        y = jnp.dot(third, w, preferred_element_type=F32)
        y = y + jnp.dot(second, w, preferred_element_type=F32)
        y = y + jnp.dot(first, w, preferred_element_type=F32)
        mine = (lane + 256 * n) // W_E == own
        y = jnp.where(mine[None], y.reshape(CHUNKS, H, 256), 0.0)
        y = jnp.sum(y, axis=1)
        out_ref[:, 2 * n, :] = y[:, :128]
        out_ref[:, 2 * n + 1, :] = y[:, 128:]
    zero = jnp.zeros((CHUNKS, 128), F32)
    out_ref[:, 6, :] = zero
    out_ref[:, 7, :] = zero


def project(parts, weight):
    return pl.pallas_call(
        project_kernel,
        out_shape=jax.ShapeDtypeStruct((CHUNKS, 8, 128), F32),
        in_specs=[pl.BlockSpec(memory_space=pltpu.VMEM)] * 2,
        out_specs=pl.BlockSpec(memory_space=pltpu.VMEM),
        compiler_params=pltpu.CompilerParams(vmem_limit_bytes=VMEM_LIMIT),
        name="project",
    )(parts, weight)


def share_kernel(sums_ref, state_ref, text_ref, out_ref):
    total = jnp.sum(sums_ref[...], axis=0)
    text = text_ref[...]
    s = lax.axis_index("s")
    quarter = text[:, 0:192]
    for q in range(1, 4):
        quarter = jnp.where(s == q, text[:, 192 * q : 192 * (q + 1)], quarter)
    lane = lax.broadcasted_iota(jnp.int32, (1, 128), 1)
    tail = jnp.concatenate([quarter[:, 128:192], jnp.zeros((1, 64), F32)], axis=1)
    tail = jnp.where(lane < 64, tail, state_ref[0:1, :])
    row = lax.broadcasted_iota(jnp.int32, (8, 128), 0)
    block = jnp.where(row < 6, total, jnp.where(row == 6, quarter[:, 0:128], tail))
    out_ref[...] = jnp.broadcast_to(block[None], out_ref.shape)


def share(sums, state, text):
    return pl.pallas_call(
        share_kernel,
        out_shape=jax.ShapeDtypeStruct((32, 8, 128), F32),
        in_specs=[pl.BlockSpec(memory_space=pltpu.VMEM)] * 3,
        out_specs=pl.BlockSpec(memory_space=pltpu.VMEM),
        compiler_params=pltpu.CompilerParams(vmem_limit_bytes=VMEM_LIMIT),
        name="share",
    )(sums, state, text)


def unit_rows(values):
    return values * lax.rsqrt(jnp.sum(values * values, axis=1, keepdims=True) + 1e-06)


def merge_kernel(parts_ref, out_ref, video_ref, rows):
    ends = [parts_ref[8 * s : 8 * (s + 1), 7, :] for s in range(4)]
    tops = [end[:, 64 : 64 + H] for end in ends]
    totals = [end[:, 80 : 80 + H] for end in ends]
    top = jnp.maximum(jnp.maximum(tops[0], tops[1]), jnp.maximum(tops[2], tops[3]))
    scales = [jnp.exp(t - top) for t in tops]
    total = sum(scale * value for scale, value in zip(scales, totals))
    scales = jnp.concatenate([scale / total for scale in scales], axis=0)
    lane = lax.broadcasted_iota(jnp.int32, (H, E), 1) // W_E
    head = lax.broadcasted_iota(jnp.int32, (H, E), 0)
    spread = jnp.where(lane == head, F32(1.0), F32(0.0))
    factors = jnp.dot(scales, spread, precision=HIGH, preferred_element_type=F32)
    pooled = jnp.zeros((8, E), F32)
    texts = []
    for s in range(4):
        mine = [parts_ref[8 * s : 8 * (s + 1), r, :] for r in range(6)]
        pooled = pooled + factors[8 * s : 8 * (s + 1)] * jnp.concatenate(mine, axis=1)
        texts += [parts_ref[8 * s : 8 * (s + 1), 6, :], ends[s][:, 0:64]]
    videos = unit_rows(pooled)
    texts = unit_rows(jnp.concatenate(texts, axis=1))
    out_ref[:, 0:8, :] = jnp.broadcast_to(videos[None], (16, 8, E))
    out_ref[:, 8:16, :] = jnp.broadcast_to(texts[None], (16, 8, E))
    rows[...] = videos
    video_ref[...] = rows[pl.ds(lax.axis_index("zl"), 1), :]


def merge(parts):
    return pl.pallas_call(
        merge_kernel,
        out_shape=(jax.ShapeDtypeStruct((16, 16, E), F32), jax.ShapeDtypeStruct((1, E), F32)),
        in_specs=[pl.BlockSpec(memory_space=pltpu.VMEM)],
        out_specs=(pl.BlockSpec(memory_space=pltpu.VMEM), pl.BlockSpec(memory_space=pltpu.VMEM)),
        scratch_shapes=[pltpu.VMEM((8, E), F32)],
        compiler_params=pltpu.CompilerParams(vmem_limit_bytes=VMEM_LIMIT),
        name="merge",
    )(parts)


def loss_kernel(scale_ref, pair_ref, mine_ref, other_ref, video_ref, text_ref, loss_ref, videos, texts, grads):
    core = lax.axis_index("c")
    here = lax.axis_index("xh") * 2 + lax.axis_index("xl")
    place = (here * 4 + lax.axis_index("y")) * 8 + lax.axis_index("zl")
    n = 256
    for ref, start in ((mine_ref, core * 128), (other_ref, (1 - core) * 128)):
        start = pl.multiple_of(start, 128)
        videos[pl.ds(start, 128), :] = ref[:, 0:8, :].reshape(128, E)
        texts[pl.ds(start, 128), :] = ref[:, 8:16, :].reshape(128, E)
    v, t = videos[...], texts[...]
    scale = scale_ref[0]
    logits = scale * lax.dot_general(
        v, t, (((1,), (1,)), ((), ())), precision=HIGH, preferred_element_type=F32
    )
    expd = jnp.exp(logits)
    row_sum = jnp.sum(expd, axis=1, keepdims=True)
    col_sum = jnp.sum(expd, axis=0, keepdims=True)
    row = lax.broadcasted_iota(jnp.int32, (n, n), 0)
    col = lax.broadcasted_iota(jnp.int32, (n, n), 1)
    row_id = 2 * (row % 128) + row // 128
    col_id = 2 * (col % 128) + col // 128
    pairs = jnp.sum(jnp.where(col == row_id, pair_ref[...].astype(F32), 0.0), axis=1, keepdims=True)
    hot = pairs == col_id.astype(F32)
    positive = jnp.sum(jnp.where(hot, logits, 0.0))
    loss_ref[0, 0] = (jnp.sum(jnp.log(row_sum)) + jnp.sum(jnp.log(col_sum)) - 2.0 * positive) / (2.0 * n)
    grad = (expd / row_sum + expd / col_sum - jnp.where(hot, F32(2.0), F32(0.0))) / (2.0 * n)
    grads[...] = grad
    own = core * 128 + place
    own_row = jnp.broadcast_to(grads[pl.ds(own, 1), :], (8, n))
    video_ref[...] = scale * jnp.dot(own_row, t, precision=HIGH, preferred_element_type=F32)[0:1, :]
    own_col = jnp.sum(jnp.where(col == own, grad, 0.0), axis=1, keepdims=True)
    text_ref[...] = scale * jnp.sum(own_col * v, axis=0, keepdims=True)


def losses(scale, pair, mine, other):
    vmem, smem = pl.BlockSpec(memory_space=pltpu.VMEM), pl.BlockSpec(memory_space=pltpu.SMEM)
    return pl.pallas_call(
        loss_kernel,
        out_shape=(
            jax.ShapeDtypeStruct((1, E), F32),
            jax.ShapeDtypeStruct((1, E), F32),
            jax.ShapeDtypeStruct((1, 1), F32),
        ),
        in_specs=[smem, vmem, vmem, vmem],
        out_specs=(vmem, vmem, smem),
        scratch_shapes=[pltpu.VMEM((256, E), F32), pltpu.VMEM((256, E), F32), pltpu.VMEM((256, 256), F32)],
        compiler_params=pltpu.CompilerParams(vmem_limit_bytes=VMEM_LIMIT),
        name="losses",
    )(scale, pair, mine, other)


def exchange(value, axes):
    return lax.all_to_all(value, axes, 0, 0, tiled=True)


def shards(tokens, query, value_weight, frames, text_feat, pair, logit_scale):
    parts, state = pool(frames, query, tokens)
    parts = exchange(parts, ("zl", "c"))
    sums = exchange(project(parts, value_weight), ("zl", "c"))
    gathered = exchange(share(sums, state, text_feat), ("s", "zl"))
    block, video_embed = merge(gathered)
    mine = exchange(block, ("xh", "xl", "y"))
    other = lax.ppermute(mine, "c", [(0, 1), (1, 0)])
    grad_video, grad_text, loss = losses(logit_scale.reshape(1), pair.reshape(1, -1), mine, other)
    return (video_embed, grad_video, grad_text, loss.reshape(()))


def solution(mesh):
    axes = ("xh", "xl", "y", "zl", "c", "s")
    fine = Mesh(mesh.devices.reshape(2, 2, 4, 8, 2, 4), axes)
    clips = axes[:5]
    return jax.shard_map(
        shards,
        mesh=fine,
        in_specs=(
            P(clips, "s", None),
            P(),
            P(("zl", "c"), None),
            P(clips),
            P(clips, None),
            P(),
            P(),
        ),
        out_specs=(P(clips, None), P(clips, None), P(clips, None), P()),
        check_vma=False,
    )
```

time: 1150 us -> 134 us (0.12)
  blocking collectives: 1100 us -> 113 us
  between operations: 20.5 us -> 1.97 us
  local copies, waits for them, and re-layouts: 15.6 us -> 2.63 us
    all_gather x3 -> x0, blocking collectives: 1070 us -> none  [the longest x1 526 us: shards(): lax.all_gather(text_unit, ('dp', 'fsdp'), axis=0, tiled=True)]
    all_to_all x0 -> x4, blocking collectives: none -> 113 us  [exchange(): return lax.all_to_all(value, axes, 0, 0, tiled=True)]
    unnamed x1 -> x0, blocking collectives: 35.1 us -> none
  transfers between devices with their start and end apart: 1 -> 1, of which waited for: 0 -> 1; matrix products, arithmetic and copies ran while one was open for 1% -> 0% of each run, Pallas kernels for 0% -> 0%
where the time goes in v1:
time: 134 us; the launch traced here: 133 us
  blocking collectives  113 us (84%)
  Pallas kernels  7.75 us (6%)
  starting transfers between devices  6.56 us (5%)
  local copies, waits for them, and re-layouts  2.63 us (2%)
  between operations  1.97 us (1%)
    all_to_all x4, blocking collectives, exchange(): return lax.all_to_all(value, axes, 0, 0, tiled=True)  113 us
    ppermute x1, starting transfers between devices, shards(): other = lax.ppermute(mine, 'c', [(0, 1), (1, 0)])  6.56 us
    pallas_call x1, Pallas kernels, pool(): pl.pallas_call(pool_kernel, out_shape=(jax.ShapeDtypeStruct((CHUNKS, H, 2...  3.5 us
  transfers between devices with their start and end apart: 1, of which 1 were waited for; matrix products, arithmetic and copies ran while one was open for 0% of the time, Pallas kernels for 0%

profile of v1, /device:TPU:1, one launch (start us, length us, event | category | flops | bytes accessed | tf_op | source)
XLA Modules:
  0.0 133.1 jit_solution(14635755792143772118)
XLA Ops:
  1.3 0.0 copy-start
  1.3 1.9 %copy-done = bf16[1,512,3200]{2,1,0:T(8,128)(2,1)S(1)} copy-done((bf16[1,512,3200]{2,1,0:T(8,128)(2,1)S(1)}, bf16[1,512,3200]{2,1,0:T(8,128)(2,1)}, u32[]{:S(2)}) %copy-start) | copy-done | bytes 3276824
  3.2 0.0 copy-start.2
  3.2 0.7 copy-done.2
  3.9 0.0 copy-start.1
  3.9 0.0 copy-start.3
  3.9 0.0 copy-start.4
  3.9 3.5 %pool.1 = (f32[16,16,256]{2,1,0:T(8,128)S(1)}, f32[8,128]{1,0:T(8,128)S(1)}) custom-call(s32[1]{0:T(128)S(6)} %copy.11.frames_ref, bf16[16,200]{1,0:T(8,128)(2,1)S(1)} %copy-done.2, bf16[1,512,3200]{2,1,0:T(8,128)(2,1)S(1)} %copy-done), custom_call_target="tpu_custom_call" | custom-call | flops 419430400 | bytes 3276800 | tf_op jit(solution)/shard_map/pool/pallas_call | solution.py:68
  7.4 33.6 %all_to_all.20.parts_ref = f32[16,16,256]{2,1,0:T(8,128)S(1)} all-to-all(f32[16,16,256]{2,1,0:T(8,128)S(1)} %get-tuple-element.11), channel_id=1, replica_groups=mesh['xh'=2,'xl'=2,'y'=4,'zl'=8,'c'=2,'s'=4] {'zl','c'}, dimensions={0} | all-to-all | bytes 524288 | tf_op jit(solution)/shard_map/all_to_all | solution.py:244
  41.1 0.0 copy-done.1
  41.1 0.5 project.1
  41.6 15.2 %all_to_all.21.sums_ref = f32[16,8,128]{2,1,0:T(8,128)S(1)} all-to-all(f32[16,8,128]{2,1,0:T(8,128)S(1)} %project.1), channel_id=1, replica_groups=mesh['xh'=2,'xl'=2,'y'=4,'zl'=8,'c'=2,'s'=4] {'zl','c'}, dimensions={0} | all-to-all | bytes 131072 | tf_op jit(solution)/shard_map/all_to_all | solution.py:244
  56.7 0.0 copy-done.3
  56.7 0.1 share.1
  56.8 47.2 %all_to_all.22.parts_ref = f32[32,8,128]{2,1,0:T(8,128)S(1)} all-to-all(f32[32,8,128]{2,1,0:T(8,128)S(1)} %share.1), channel_id=1, replica_groups=mesh['xh'=2,'xl'=2,'y'=4,'zl'=8,'c'=2,'s'=4] {'s','zl'}, dimensions={0} | all-to-all | bytes 262144 | tf_op jit(solution)/shard_map/all_to_all | solution.py:244
  104.1 1.1 merge.1
  105.2 16.9 %all_to_all.23.mine_ref = f32[16,16,768]{2,1,0:T(8,128)S(1)} all-to-all(f32[16,16,768]{2,1,0:T(8,128)S(1)} %get-tuple-element.14), channel_id=1, replica_groups=mesh['xh'=2,'xl'=2,'y'=4,'zl'=8,'c'=2,'s'=4] {'xh','xl','y'}, dimensions={0} | all-to-all | bytes 1572864 | tf_op jit(solution)/shard_map/all_to_all | solution.py:244
  122.1 6.6 %collective-permute-start = (f32[16,16,768]{2,1,0:T(8,128)S(1)}, f32[16,16,768]{2,1,0:T(8,128)S(1)}, u32[]{:S(2)}, u32[]{:S(2)}) collective-permute-start(f32[16,16,768]{2,1,0:T(8,128)S(1)} %all_to_all.23.mine_ref), channel_id=1, source_target_pairs={{0,4},{4,0},{1,5},{5,1},{2,6},{6,2},{3,7},{7,3},{8,12},{12,8},{9,1... | collective-permute-start | bytes 2359304 | tf_op jit(solution)/shard_map/ppermute | solution.py:254
  129.3 1.2 collective-permute-done.other_ref
  130.6 0.0 copy-done.4
  130.6 2.6 %losses.1 = (f32[1,768]{1,0:T(1,128)}, f32[1,768]{1,0:T(1,128)}, f32[1,1]{1,0:T(1,128)}) custom-call(f32[1]{0:T(128)} %bitcast.3.scale_ref, s32[1,256]{1,0:T(1,128)S(1)} %bitcast.4, f32[16,16,768]{2,1,0:T(8,128)S(1)} %all_to_all.23.mine_ref, f32[16,16,768]{2,1,0:T(8,128)S(1)} %collective-permute-done.other_ref), custom_call_target="tpu_custom_call" | custom-call | tf_op jit(solution)/shard_map/losses/pallas_call | solution.py:228
Async XLA Ops:
  1.3 1.9 %copy-start = (bf16[1,512,3200]{2,1,0:T(8,128)(2,1)S(1)}, bf16[1,512,3200]{2,1,0:T(8,128)(2,1)}, u32[]{:S(2)}) copy-start(bf16[1,512,3200]{2,1,0:T(8,128)(2,1)} %tok_hbm.1) | copy-start | bytes 9830404
  3.2 0.7 copy-start.2
  3.9 37.2 %copy-start.1 = (bf16[200,768]{1,0:T(8,128)(2,1)S(1)}, bf16[200,768]{1,0:T(8,128)(2,1)}, u32[]{:S(2)}) copy-start(bf16[200,768]{1,0:T(8,128)(2,1)} %weight_ref.1) | copy-start | bytes 921604
  3.9 52.8 %copy-start.3 = (f32[1,768]{1,0:T(1,128)S(1)}, f32[1,768]{1,0:T(1,128)}, u32[]{:S(2)}) copy-start(f32[1,768]{1,0:T(1,128)} %text_ref.1) | copy-start | bytes 9220
  3.9 126.7 %copy-start.4 = (s32[256]{0:T(256)S(1)}, s32[256]{0:T(256)}, u32[]{:S(2)}) copy-start(s32[256]{0:T(256)} %param.12) | copy-start | bytes 3076
  122.1 8.5 %collective-permute-start = (f32[16,16,768]{2,1,0:T(8,128)S(1)}, f32[16,16,768]{2,1,0:T(8,128)S(1)}, u32[]{:S(2)}, u32[]{:S(2)}) collective-permute-start(f32[16,16,768]{2,1,0:T(8,128)S(1)} %all_to_all.23.mine_ref), channel_id=1, source_target_pairs={{0,4},{4,0},{1,5},{5,1},{2,6},{6,2},{3,7},{7,3},{8,12},{12,8},{9,1... | collective-permute-start | bytes 2359304 | tf_op jit(solution)/shard_map/ppermute | solution.py:254

commit v2 on v1

--- a/solution.py
+++ b/solution.py
@@ -15,6 +15,11 @@
 HIGH = lax.Precision.HIGHEST
 F32, BF16 = jnp.float32, jnp.bfloat16
 VMEM_LIMIT = 40 * 1024 * 1024
+GROUP = ("xl", "y", "c")
+
+
+def chunk_of(m, zl):
+    return (((zl >> 2) ^ (zl & 1) ^ (m >> 2)) << 2) | ((zl ^ m) & 3)
 
 
 def three_terms(value):
@@ -25,13 +30,8 @@
     return first, second, third
 
 
-def pool_kernel(frames_ref, query_ref, tok_hbm, parts_ref, state_ref, tok, spread, mixed, sems):
-    copies = [
-        pltpu.make_async_copy(tok_hbm.at[0, pl.ds(FT * j, FT)], tok.at[pl.ds(FT * j, FT)], sems.at[j])
-        for j in range(FRAMES_HERE)
-    ]
-    for copy in copies:
-        copy.start()
+def pool_kernel(frames_ref, query_ref, tok_ref, parts_ref, state_ref, spread, mixed):
+    tok = tok_ref.at[0]
     spread[...] = jnp.zeros_like(spread)
     rows = query_ref[...].astype(F32)
     for h in range(H):
@@ -40,7 +40,6 @@
     used = frames_ref[0] - lax.axis_index("s") * FRAMES_HERE
     scores = []
     for j in range(FRAMES_HERE):
-        copies[j].wait()
         part = lax.dot_general(
             heads_q, tok[FT * j : FT * (j + 1), :], (((1,), (1,)), ((), ())), preferred_element_type=F32
         )
@@ -56,8 +55,11 @@
         cols = slice(step * n, step * (n + 1))
         out = jnp.dot(terms, tok[:, cols], preferred_element_type=F32)
         mixed[:, cols] = (out[2 * H :] + out[H : 2 * H]) + out[:H]
+    zl = lax.axis_index("zl")
     for k in range(CHUNKS):
-        parts_ref[k, :, 0:ROWS] = mixed[:, ROWS * k : ROWS * (k + 1)]
+        pair = k // 2
+        member = (((pair >> 2) ^ (zl >> 2) ^ (zl & 1)) << 2) | ((pair ^ zl) & 3)
+        parts_ref[2 * member + k % 2, :, 0:ROWS] = mixed[:, ROWS * k : ROWS * (k + 1)]
     lane = lax.broadcasted_iota(jnp.int32, (H, 128), 1)
     head = lax.broadcasted_iota(jnp.int32, (H, 128), 0)
     row = jnp.where(lane == 64 + head, top, 0.0) + jnp.where(lane == 80 + head, total, 0.0)
@@ -74,14 +76,12 @@
         in_specs=[
             pl.BlockSpec(memory_space=pltpu.SMEM),
             pl.BlockSpec(memory_space=pltpu.VMEM),
-            pl.BlockSpec(memory_space=pl.ANY),
+            pl.BlockSpec(memory_space=pltpu.VMEM),
         ],
         out_specs=(pl.BlockSpec(memory_space=pltpu.VMEM), pl.BlockSpec(memory_space=pltpu.VMEM)),
         scratch_shapes=[
-            pltpu.VMEM((TOK, D), BF16),
             pltpu.VMEM((H, D), F32),
             pltpu.VMEM((H, D), F32),
-            pltpu.SemaphoreType.DMA((FRAMES_HERE,)),
         ],
         compiler_params=pltpu.CompilerParams(vmem_limit_bytes=VMEM_LIMIT),
         cost_estimate=pl.CostEstimate(flops=4 * 64 * TOK * D, bytes_accessed=TOK * D * 2, transcendentals=H * TOK),
@@ -121,72 +121,69 @@
     )(parts, weight)
 
 
-def share_kernel(sums_ref, state_ref, text_ref, out_ref):
+def share_kernel(sums_ref, state_ref, out_ref):
     total = jnp.sum(sums_ref[...], axis=0)
-    text = text_ref[...]
-    s = lax.axis_index("s")
-    quarter = text[:, 0:192]
-    for q in range(1, 4):
-        quarter = jnp.where(s == q, text[:, 192 * q : 192 * (q + 1)], quarter)
-    lane = lax.broadcasted_iota(jnp.int32, (1, 128), 1)
-    tail = jnp.concatenate([quarter[:, 128:192], jnp.zeros((1, 64), F32)], axis=1)
-    tail = jnp.where(lane < 64, tail, state_ref[0:1, :])
     row = lax.broadcasted_iota(jnp.int32, (8, 128), 0)
-    block = jnp.where(row < 6, total, jnp.where(row == 6, quarter[:, 0:128], tail))
+    block = jnp.where(row < 6, total, state_ref[...])
     out_ref[...] = jnp.broadcast_to(block[None], out_ref.shape)
 
 
-def share(sums, state, text):
+def share(sums, state):
     return pl.pallas_call(
         share_kernel,
-        out_shape=jax.ShapeDtypeStruct((32, 8, 128), F32),
-        in_specs=[pl.BlockSpec(memory_space=pltpu.VMEM)] * 3,
+        out_shape=jax.ShapeDtypeStruct((4, 8, 128), F32),
+        in_specs=[pl.BlockSpec(memory_space=pltpu.VMEM)] * 2,
         out_specs=pl.BlockSpec(memory_space=pltpu.VMEM),
         compiler_params=pltpu.CompilerParams(vmem_limit_bytes=VMEM_LIMIT),
         name="share",
-    )(sums, state, text)
+    )(sums, state)
 
 
 def unit_rows(values):
     return values * lax.rsqrt(jnp.sum(values * values, axis=1, keepdims=True) + 1e-06)
 
 
-def merge_kernel(parts_ref, out_ref, video_ref, rows):
-    ends = [parts_ref[8 * s : 8 * (s + 1), 7, :] for s in range(4)]
-    tops = [end[:, 64 : 64 + H] for end in ends]
-    totals = [end[:, 80 : 80 + H] for end in ends]
-    top = jnp.maximum(jnp.maximum(tops[0], tops[1]), jnp.maximum(tops[2], tops[3]))
-    scales = [jnp.exp(t - top) for t in tops]
-    total = sum(scale * value for scale, value in zip(scales, totals))
-    scales = jnp.concatenate([scale / total for scale in scales], axis=0)
+def combine_kernel(parts_ref, text_ref, out_ref, video_ref):
+    ends = parts_ref[:, 7, :]
+    tops, totals = ends[:, 64 : 64 + H], ends[:, 80 : 80 + H]
+    scales = jnp.exp(tops - jnp.max(tops, axis=0, keepdims=True))
+    scales = scales / jnp.sum(scales * totals, axis=0, keepdims=True)
     lane = lax.broadcasted_iota(jnp.int32, (H, E), 1) // W_E
     head = lax.broadcasted_iota(jnp.int32, (H, E), 0)
     spread = jnp.where(lane == head, F32(1.0), F32(0.0))
     factors = jnp.dot(scales, spread, precision=HIGH, preferred_element_type=F32)
-    pooled = jnp.zeros((8, E), F32)
-    texts = []
-    for s in range(4):
-        mine = [parts_ref[8 * s : 8 * (s + 1), r, :] for r in range(6)]
-        pooled = pooled + factors[8 * s : 8 * (s + 1)] * jnp.concatenate(mine, axis=1)
-        texts += [parts_ref[8 * s : 8 * (s + 1), 6, :], ends[s][:, 0:64]]
-    videos = unit_rows(pooled)
-    texts = unit_rows(jnp.concatenate(texts, axis=1))
-    out_ref[:, 0:8, :] = jnp.broadcast_to(videos[None], (16, 8, E))
-    out_ref[:, 8:16, :] = jnp.broadcast_to(texts[None], (16, 8, E))
-    rows[...] = videos
-    video_ref[...] = rows[pl.ds(lax.axis_index("zl"), 1), :]
-
-
-def merge(parts):
-    return pl.pallas_call(
-        merge_kernel,
-        out_shape=(jax.ShapeDtypeStruct((16, 16, E), F32), jax.ShapeDtypeStruct((1, E), F32)),
+    values = jnp.concatenate([parts_ref[:, r, :] for r in range(6)], axis=1)
+    video = unit_rows(jnp.sum(factors * values, axis=0, keepdims=True))
+    video_ref[...] = video
+    out_ref[:, 0, :] = jnp.broadcast_to(video, (8, E))
+    out_ref[:, 1, :] = jnp.broadcast_to(unit_rows(text_ref[...]), (8, E))
+
+
+def combine(parts, text):
+    return pl.pallas_call(
+        combine_kernel,
+        out_shape=(jax.ShapeDtypeStruct((8, 2, E), F32), jax.ShapeDtypeStruct((1, E), F32)),
+        in_specs=[pl.BlockSpec(memory_space=pltpu.VMEM)] * 2,
+        out_specs=(pl.BlockSpec(memory_space=pltpu.VMEM), pl.BlockSpec(memory_space=pltpu.VMEM)),
+        compiler_params=pltpu.CompilerParams(vmem_limit_bytes=VMEM_LIMIT),
+        name="combine",
+    )(parts, text)
+
+
+def repeat_kernel(rows_ref, out_ref):
+    out_ref[:, 0:8, :] = jnp.broadcast_to(rows_ref[:, 0, :][None], (16, 8, E))
+    out_ref[:, 8:16, :] = jnp.broadcast_to(rows_ref[:, 1, :][None], (16, 8, E))
+
+
+def repeat(rows):
+    return pl.pallas_call(
+        repeat_kernel,
+        out_shape=jax.ShapeDtypeStruct((16, 16, E), F32),
         in_specs=[pl.BlockSpec(memory_space=pltpu.VMEM)],
-        out_specs=(pl.BlockSpec(memory_space=pltpu.VMEM), pl.BlockSpec(memory_space=pltpu.VMEM)),
-        scratch_shapes=[pltpu.VMEM((8, E), F32)],
-        compiler_params=pltpu.CompilerParams(vmem_limit_bytes=VMEM_LIMIT),
-        name="merge",
-    )(parts)
+        out_specs=pl.BlockSpec(memory_space=pltpu.VMEM),
+        compiler_params=pltpu.CompilerParams(vmem_limit_bytes=VMEM_LIMIT),
+        name="repeat",
+    )(rows)
 
 
 def loss_kernel(scale_ref, pair_ref, mine_ref, other_ref, video_ref, text_ref, loss_ref, videos, texts, grads):
@@ -245,12 +242,17 @@
 
 
 def shards(tokens, query, value_weight, frames, text_feat, pair, logit_scale):
+    moves = [
+        ((m * 8) + chunk_of(m, zl), m * 8 + zl)
+        for m in range(8)
+        for zl in range(8)
+    ]
+    weight = lax.ppermute(value_weight, ("xl", "y", "zl"), moves)
     parts, state = pool(frames, query, tokens)
-    parts = exchange(parts, ("zl", "c"))
-    sums = exchange(project(parts, value_weight), ("zl", "c"))
-    gathered = exchange(share(sums, state, text_feat), ("s", "zl"))
-    block, video_embed = merge(gathered)
-    mine = exchange(block, ("xh", "xl", "y"))
+    parts = exchange(parts, GROUP)
+    sums = exchange(project(parts, weight), GROUP)
+    rows, video_embed = combine(exchange(share(sums, state), "s"), text_feat)
+    mine = exchange(repeat(exchange(rows, "zl")), ("xh", "xl", "y"))
     other = lax.ppermute(mine, "c", [(0, 1), (1, 0)])
     grad_video, grad_text, loss = losses(logit_scale.reshape(1), pair.reshape(1, -1), mine, other)
     return (video_embed, grad_video, grad_text, loss.reshape(()))

time: 134 us -> 129 us (0.963)
  blocking collectives: 113 us -> 109 us
  Pallas kernels: 7.75 us -> 5.99 us
  starting transfers between devices: 6.56 us -> 8.26 us
    all_to_all x4 -> x5, blocking collectives: 113 us -> 109 us  [exchange(): return lax.all_to_all(value, axes, 0, 0, tiled=True)]
    pallas_call x1, Pallas kernels: 3.5 us -> 1.81 us  [pool(): pl.pallas_call(pool_kernel, out_shape=(jax.ShapeDtypeStruct((CHUNKS, H, 2...]
    ppermute x0 -> x1, starting transfers between devices: none -> 1.62 us  [shards(): weight = lax.ppermute(value_weight, ('xl', 'y', 'zl'), moves)]
  transfers between devices with their start and end apart: 1 -> 2, of which waited for: 1 -> 1; matrix products, arithmetic and copies ran while one was open for 0% -> 0% of each run, Pallas kernels for 0% -> 1%
where the time goes in v2:
time: 129 us
  blocking collectives  109 us (84%)
  starting transfers between devices  8.26 us (6%)
  Pallas kernels  5.99 us (5%)
  local copies, waits for them, and re-layouts  2.62 us (2%)
  between operations  1.98 us (2%)
    all_to_all x5, blocking collectives, exchange(): return lax.all_to_all(value, axes, 0, 0, tiled=True)  109 us
    ppermute x1, starting transfers between devices, shards(): other = lax.ppermute(mine, 'c', [(0, 1), (1, 0)])  6.63 us
    unnamed x8, local copies, waits for them, and re-layouts  2.62 us
  transfers between devices with their start and end apart: 2, of which 1 were waited for; matrix products, arithmetic and copies ran while one was open for 0% of the time, Pallas kernels for 1%

profile of v2, /device:TPU:1, one launch (start us, length us, event | category | flops | bytes accessed | tf_op | source)
XLA Modules:
  0.0 128.7 jit_solution(6419728002847644326)
XLA Ops:
  0.6 1.6 %collective-permute-start = (bf16[200,768]{1,0:T(8,128)(2,1)}, bf16[200,768]{1,0:T(8,128)(2,1)S(1)}, u32[]{:S(2)}, u32[]{:S(2)}) collective-permute-start(bf16[200,768]{1,0:T(8,128)(2,1)} %param.9), channel_id=1, source_target_pairs={{0,0},{40,8},{16,16},{56,24},{32,32},{8,40},{48,48},{24,56},{72,64... | collective-permute-start | bytes 921608 | tf_op jit(solution)/shard_map/ppermute | solution.py:250
  2.9 0.0 copy-start
  2.9 1.9 %copy-done = bf16[1,512,3200]{2,1,0:T(8,128)(2,1)S(1)} copy-done((bf16[1,512,3200]{2,1,0:T(8,128)(2,1)S(1)}, bf16[1,512,3200]{2,1,0:T(8,128)(2,1)}, u32[]{:S(2)}) %copy-start) | copy-done | bytes 3276824
  4.8 0.0 copy-start.1
  4.8 0.7 copy-done.1
  5.5 0.0 copy-start.2
  5.5 0.0 copy-start.3
  5.5 1.8 %pool.1 = (f32[16,16,256]{2,1,0:T(8,128)S(1)}, f32[8,128]{1,0:T(8,128)S(1)}) custom-call(s32[1]{0:T(128)S(6)} %copy.11.frames_ref, bf16[16,200]{1,0:T(8,128)(2,1)S(1)} %copy-done.1, bf16[1,512,3200]{2,1,0:T(8,128)(2,1)S(1)} %copy-done), custom_call_target="tpu_custom_call" | custom-call | flops 419430400 | bytes 3276800 | tf_op jit(solution)/shard_map/pool/pallas_call | solution.py:70
  7.4 24.3 %all_to_all.25.parts_ref = f32[16,16,256]{2,1,0:T(8,128)S(1)} all-to-all(f32[16,16,256]{2,1,0:T(8,128)S(1)} %get-tuple-element.11), channel_id=1, replica_groups=mesh['xh'=2,'xl'=2,'y'=4,'zl'=8,'c'=2,'s'=4] {'xl','y','c'}, dimensions={0} | all-to-all | bytes 524288 | tf_op jit(solution)/shard_map/all_to_all | solution.py:241
  31.7 0.0 collective-permute-done.weight_ref
  31.7 0.5 project.1
  32.2 9.3 %all_to_all.26.sums_ref = f32[16,8,128]{2,1,0:T(8,128)S(1)} all-to-all(f32[16,8,128]{2,1,0:T(8,128)S(1)} %project.1), channel_id=1, replica_groups=mesh['xh'=2,'xl'=2,'y'=4,'zl'=8,'c'=2,'s'=4] {'xl','y','c'}, dimensions={0} | all-to-all | bytes 131072 | tf_op jit(solution)/shard_map/all_to_all | solution.py:241
  41.5 42.0 %all_to_all.27.parts_ref = f32[4,8,128]{2,1,0:T(8,128)S(1)} all-to-all(f32[4,8,128]{2,1,0:T(8,128)S(1)} %share.1), channel_id=1, replica_groups=mesh['xh'=2,'xl'=2,'y'=4,'zl'=8,'c'=2,'s'=4] {'s'}, dimensions={0} | all-to-all | bytes 32768 | tf_op jit(solution)/shard_map/all_to_all | solution.py:241
  83.5 0.0 copy-done.2
  83.5 1.0 combine.1
  84.5 18.3 %all_to_all.28.rows_ref = f32[8,2,768]{2,1,0:T(2,128)S(1)} all-to-all(f32[8,2,768]{2,1,0:T(2,128)S(1)} %get-tuple-element.14), channel_id=1, replica_groups=mesh['xh'=2,'xl'=2,'y'=4,'zl'=8,'c'=2,'s'=4] {'zl'}, dimensions={0} | all-to-all | bytes 98304 | tf_op jit(solution)/shard_map/all_to_all | solution.py:241
  102.8 0.1 repeat.1
  102.9 14.7 %all_to_all.29.mine_ref = f32[16,16,768]{2,1,0:T(8,128)S(1)} all-to-all(f32[16,16,768]{2,1,0:T(8,128)S(1)} %repeat.1), channel_id=1, replica_groups=mesh['xh'=2,'xl'=2,'y'=4,'zl'=8,'c'=2,'s'=4] {'xh','xl','y'}, dimensions={0} | all-to-all | bytes 1572864 | tf_op jit(solution)/shard_map/all_to_all | solution.py:241
  117.6 6.6 %collective-permute-start.1 = (f32[16,16,768]{2,1,0:T(8,128)S(1)}, f32[16,16,768]{2,1,0:T(8,128)S(1)}, u32[]{:S(2)}, u32[]{:S(2)}) collective-permute-start(f32[16,16,768]{2,1,0:T(8,128)S(1)} %all_to_all.29.mine_ref), channel_id=1, source_target_pairs={{0,4},{4,0},{1,5},{5,1},{2,6},{6,2},{3,7},{7,3},{8,12},{12,8},{9,1... | collective-permute-start | bytes 2359304 | tf_op jit(solution)/shard_map/ppermute | solution.py:256
  124.8 1.2 collective-permute-done.1.other_ref
  126.1 0.0 copy-done.3
  126.1 2.6 %losses.1 = (f32[1,768]{1,0:T(1,128)}, f32[1,768]{1,0:T(1,128)}, f32[1,1]{1,0:T(1,128)}) custom-call(f32[1]{0:T(128)} %bitcast.3.scale_ref, s32[1,256]{1,0:T(1,128)S(1)} %bitcast.4, f32[16,16,768]{2,1,0:T(8,128)S(1)} %all_to_all.29.mine_ref, f32[16,16,768]{2,1,0:T(8,128)S(1)} %collective-permute-done.1.other_ref), custom_call_target="tpu_custom_call" | custom-call | tf_op jit(solution)/shard_map/losses/pallas_call | solution.py:225
  (1 shorter events, 0.0 us)
Async XLA Ops:
  0.6 31.0 %collective-permute-start = (bf16[200,768]{1,0:T(8,128)(2,1)}, bf16[200,768]{1,0:T(8,128)(2,1)S(1)}, u32[]{:S(2)}, u32[]{:S(2)}) collective-permute-start(bf16[200,768]{1,0:T(8,128)(2,1)} %param.9), channel_id=1, source_target_pairs={{0,0},{40,8},{16,16},{56,24},{32,32},{8,40},{48,48},{24,56},{72,64... | collective-permute-start | bytes 921608 | tf_op jit(solution)/shard_map/ppermute | solution.py:250
  2.9 1.9 %copy-start = (bf16[1,512,3200]{2,1,0:T(8,128)(2,1)S(1)}, bf16[1,512,3200]{2,1,0:T(8,128)(2,1)}, u32[]{:S(2)}) copy-start(bf16[1,512,3200]{2,1,0:T(8,128)(2,1)} %tok_ref.1) | copy-start | bytes 9830404
  4.8 0.7 copy-start.1
  5.5 78.0 %copy-start.2 = (f32[1,768]{1,0:T(1,128)S(1)}, f32[1,768]{1,0:T(1,128)}, u32[]{:S(2)}) copy-start(f32[1,768]{1,0:T(1,128)} %text_ref.1) | copy-start | bytes 9220
  5.5 120.6 %copy-start.3 = (s32[256]{0:T(256)S(1)}, s32[256]{0:T(256)}, u32[]{:S(2)}) copy-start(s32[256]{0:T(256)} %param.12) | copy-start | bytes 3076
  117.6 8.5 %collective-permute-start.1 = (f32[16,16,768]{2,1,0:T(8,128)S(1)}, f32[16,16,768]{2,1,0:T(8,128)S(1)}, u32[]{:S(2)}, u32[]{:S(2)}) collective-permute-start(f32[16,16,768]{2,1,0:T(8,128)S(1)} %all_to_all.29.mine_ref), channel_id=1, source_target_pairs={{0,4},{4,0},{1,5},{5,1},{2,6},{6,2},{3,7},{7,3},{8,12},{12,8},{9,1... | collective-permute-start | bytes 2359304 | tf_op jit(solution)/shard_map/ppermute | solution.py:256

commit v3 on v1

--- a/solution.py
+++ b/solution.py
@@ -15,6 +15,12 @@
 HIGH = lax.Precision.HIGHEST
 F32, BF16 = jnp.float32, jnp.bfloat16
 VMEM_LIMIT = 40 * 1024 * 1024
+POOL_LIMIT = 52 * 1024 * 1024
+GROUP = ("xl", "y", "c")
+
+
+def chunk_of(m, zl):
+    return (((zl >> 2) ^ (zl & 1) ^ (m >> 2)) << 2) | ((zl ^ m) & 3)
 
 
 def three_terms(value):
@@ -25,7 +31,9 @@
     return first, second, third
 
 
-def pool_kernel(frames_ref, query_ref, tok_hbm, parts_ref, state_ref, tok, spread, mixed, sems):
+def pool_kernel(frames_ref, query_hbm, tok_hbm, parts_ref, state_ref, tok, query_ref, spread, mixed, sems):
+    query_copy = pltpu.make_async_copy(query_hbm, query_ref, sems.at[FRAMES_HERE])
+    query_copy.start()
     copies = [
         pltpu.make_async_copy(tok_hbm.at[0, pl.ds(FT * j, FT)], tok.at[pl.ds(FT * j, FT)], sems.at[j])
         for j in range(FRAMES_HERE)
@@ -33,6 +41,7 @@
     for copy in copies:
         copy.start()
     spread[...] = jnp.zeros_like(spread)
+    query_copy.wait()
     rows = query_ref[...].astype(F32)
     for h in range(H):
         spread[h : h + 1, W_H * h : W_H * (h + 1)] = rows[h : h + 1, :]
@@ -56,8 +65,11 @@
         cols = slice(step * n, step * (n + 1))
         out = jnp.dot(terms, tok[:, cols], preferred_element_type=F32)
         mixed[:, cols] = (out[2 * H :] + out[H : 2 * H]) + out[:H]
+    zl = lax.axis_index("zl")
     for k in range(CHUNKS):
-        parts_ref[k, :, 0:ROWS] = mixed[:, ROWS * k : ROWS * (k + 1)]
+        pair = k // 2
+        member = (((pair >> 2) ^ (zl >> 2) ^ (zl & 1)) << 2) | ((pair ^ zl) & 3)
+        parts_ref[2 * member + k % 2, :, 0:ROWS] = mixed[:, ROWS * k : ROWS * (k + 1)]
     lane = lax.broadcasted_iota(jnp.int32, (H, 128), 1)
     head = lax.broadcasted_iota(jnp.int32, (H, 128), 0)
     row = jnp.where(lane == 64 + head, top, 0.0) + jnp.where(lane == 80 + head, total, 0.0)
@@ -73,17 +85,18 @@
         ),
         in_specs=[
             pl.BlockSpec(memory_space=pltpu.SMEM),
-            pl.BlockSpec(memory_space=pltpu.VMEM),
+            pl.BlockSpec(memory_space=pl.ANY),
             pl.BlockSpec(memory_space=pl.ANY),
         ],
         out_specs=(pl.BlockSpec(memory_space=pltpu.VMEM), pl.BlockSpec(memory_space=pltpu.VMEM)),
         scratch_shapes=[
             pltpu.VMEM((TOK, D), BF16),
+            pltpu.VMEM((H, W_H), BF16),
             pltpu.VMEM((H, D), F32),
             pltpu.VMEM((H, D), F32),
-            pltpu.SemaphoreType.DMA((FRAMES_HERE,)),
+            pltpu.SemaphoreType.DMA((FRAMES_HERE + 1,)),
         ],
-        compiler_params=pltpu.CompilerParams(vmem_limit_bytes=VMEM_LIMIT),
+        compiler_params=pltpu.CompilerParams(vmem_limit_bytes=POOL_LIMIT),
         cost_estimate=pl.CostEstimate(flops=4 * 64 * TOK * D, bytes_accessed=TOK * D * 2, transcendentals=H * TOK),
         name="pool",
     )(frames, query, tokens)
@@ -245,9 +258,15 @@
 
 
 def shards(tokens, query, value_weight, frames, text_feat, pair, logit_scale):
+    moves = [
+        ((m * 8) + chunk_of(m, zl), m * 8 + zl)
+        for m in range(8)
+        for zl in range(8)
+    ]
+    weight = lax.ppermute(value_weight, ("xl", "y", "zl"), moves)
     parts, state = pool(frames, query, tokens)
-    parts = exchange(parts, ("zl", "c"))
-    sums = exchange(project(parts, value_weight), ("zl", "c"))
+    parts = exchange(parts, GROUP)
+    sums = exchange(project(parts, weight), GROUP)
     gathered = exchange(share(sums, state, text_feat), ("s", "zl"))
     block, video_embed = merge(gathered)
     mine = exchange(block, ("xh", "xl", "y"))

time: 134 us -> 124 us (0.925)
  blocking collectives: 113 us -> 103 us
  local copies, waits for them, and re-layouts: 2.63 us -> 0.7 us
    all_to_all x4, blocking collectives: 113 us -> 103 us  [exchange(): return lax.all_to_all(value, axes, 0, 0, tiled=True)]
    unnamed x10 -> x6, local copies, waits for them, and re-layouts: 2.63 us -> 0.7 us
    ppermute x0 -> x1, starting transfers between devices: none -> 1.62 us  [shards(): weight = lax.ppermute(value_weight, ('xl', 'y', 'zl'), moves)]
  transfers between devices with their start and end apart: 1 -> 2, of which waited for: 1 -> 1; matrix products, arithmetic and copies ran while one was open for 0% -> 0% of each run, Pallas kernels for 0% -> 3%
where the time goes in v3:
time: 124 us; the launch traced here: 123 us
  blocking collectives  103 us (83%)
  Pallas kernels  8.46 us (7%)
  starting transfers between devices  7.87 us (6%)
  between operations  1.97 us (2%)
  waiting for transfers between devices  1.25 us (1%)
    all_to_all x4, blocking collectives, exchange(): return lax.all_to_all(value, axes, 0, 0, tiled=True)  103 us
    ppermute x1, starting transfers between devices, shards(): other = lax.ppermute(mine, 'c', [(0, 1), (1, 0)])  6.25 us
    pallas_call x1, Pallas kernels, pool(): pl.pallas_call(pool_kernel, out_shape=(jax.ShapeDtypeStruct((CHUNKS, H, 2...  4.21 us
    pallas_call x1, Pallas kernels, losses(): pl.pallas_call(loss_kernel, out_shape=(jax.ShapeDtypeStruct((1, E), F32),...  2.57 us
  transfers between devices with their start and end apart: 2, of which 1 were waited for; matrix products, arithmetic and copies ran while one was open for 0% of the time, Pallas kernels for 3%

profile of v3, /device:TPU:1, one launch (start us, length us, event | category | flops | bytes accessed | tf_op | source)
XLA Modules:
  0.0 123.4 jit_solution(2523273810484724524)
XLA Ops:
  0.6 1.6 %collective-permute-start = (bf16[200,768]{1,0:T(8,128)(2,1)}, bf16[200,768]{1,0:T(8,128)(2,1)S(1)}, u32[]{:S(2)}, u32[]{:S(2)}) collective-permute-start(bf16[200,768]{1,0:T(8,128)(2,1)} %param.9), channel_id=1, source_target_pairs={{0,0},{40,8},{16,16},{56,24},{32,32},{8,40},{48,48},{24,56},{72,64... | collective-permute-start | bytes 921608 | tf_op jit(solution)/shard_map/ppermute | solution.py:266
  2.9 0.0 copy-start
  2.9 0.7 copy-done
  3.6 0.0 copy-start.1
  3.6 0.0 copy-start.2
  3.6 4.2 %pool.1 = (f32[16,16,256]{2,1,0:T(8,128)S(1)}, f32[8,128]{1,0:T(8,128)S(1)}) custom-call(s32[1]{0:T(128)S(6)} %copy.11.frames_ref, bf16[16,200]{1,0:T(8,128)(2,1)S(1)} %copy-done, bf16[1,512,3200]{2,1,0:T(8,128)(2,1)} %tok_hbm.1), custom_call_target="tpu_custom_call" | custom-call | flops 419430400 | bytes 3276800 | tf_op jit(solution)/shard_map/pool/pallas_call | solution.py:80
  7.8 24.3 %all_to_all.20.parts_ref = f32[16,16,256]{2,1,0:T(8,128)S(1)} all-to-all(f32[16,16,256]{2,1,0:T(8,128)S(1)} %get-tuple-element.11), channel_id=1, replica_groups=mesh['xh'=2,'xl'=2,'y'=4,'zl'=8,'c'=2,'s'=4] {'xl','y','c'}, dimensions={0} | all-to-all | bytes 524288 | tf_op jit(solution)/shard_map/all_to_all | solution.py:257
  32.1 0.0 collective-permute-done.weight_ref
  32.1 0.5 project.1
  32.6 9.3 %all_to_all.21.sums_ref = f32[16,8,128]{2,1,0:T(8,128)S(1)} all-to-all(f32[16,8,128]{2,1,0:T(8,128)S(1)} %project.1), channel_id=1, replica_groups=mesh['xh'=2,'xl'=2,'y'=4,'zl'=8,'c'=2,'s'=4] {'xl','y','c'}, dimensions={0} | all-to-all | bytes 131072 | tf_op jit(solution)/shard_map/all_to_all | solution.py:257
  41.9 0.0 copy-done.1
  41.9 0.1 share.1
  42.0 54.5 %all_to_all.22.parts_ref = f32[32,8,128]{2,1,0:T(8,128)S(1)} all-to-all(f32[32,8,128]{2,1,0:T(8,128)S(1)} %share.1), channel_id=1, replica_groups=mesh['xh'=2,'xl'=2,'y'=4,'zl'=8,'c'=2,'s'=4] {'s','zl'}, dimensions={0} | all-to-all | bytes 262144 | tf_op jit(solution)/shard_map/all_to_all | solution.py:257
  96.5 1.1 merge.1
  97.6 15.1 %all_to_all.23.mine_ref = f32[16,16,768]{2,1,0:T(8,128)S(1)} all-to-all(f32[16,16,768]{2,1,0:T(8,128)S(1)} %get-tuple-element.14), channel_id=1, replica_groups=mesh['xh'=2,'xl'=2,'y'=4,'zl'=8,'c'=2,'s'=4] {'xh','xl','y'}, dimensions={0} | all-to-all | bytes 1572864 | tf_op jit(solution)/shard_map/all_to_all | solution.py:257
  112.7 6.2 %collective-permute-start.1 = (f32[16,16,768]{2,1,0:T(8,128)S(1)}, f32[16,16,768]{2,1,0:T(8,128)S(1)}, u32[]{:S(2)}, u32[]{:S(2)}) collective-permute-start(f32[16,16,768]{2,1,0:T(8,128)S(1)} %all_to_all.23.mine_ref), channel_id=1, source_target_pairs={{0,4},{4,0},{1,5},{5,1},{2,6},{6,2},{3,7},{7,3},{8,12},{12,8},{9,1... | collective-permute-start | bytes 2359304 | tf_op jit(solution)/shard_map/ppermute | solution.py:273
  119.6 1.2 %collective-permute-done.1.other_ref = f32[16,16,768]{2,1,0:T(8,128)S(1)} collective-permute-done((f32[16,16,768]{2,1,0:T(8,128)S(1)}, f32[16,16,768]{2,1,0:T(8,128)S(1)}, u32[]{:S(2)}, u32[]{:S(2)}) %collective-permute-start.1) | collective-permute-done | bytes 786464 | tf_op jit(solution)/shard_map/ppermute | solution.py:273
  120.9 0.0 copy-done.2
  120.9 2.6 %losses.1 = (f32[1,768]{1,0:T(1,128)}, f32[1,768]{1,0:T(1,128)}, f32[1,1]{1,0:T(1,128)}) custom-call(f32[1]{0:T(128)} %bitcast.3.scale_ref, s32[1,256]{1,0:T(1,128)S(1)} %bitcast.4, f32[16,16,768]{2,1,0:T(8,128)S(1)} %all_to_all.23.mine_ref, f32[16,16,768]{2,1,0:T(8,128)S(1)} %collective-permute-done.1.other_ref), custom_call_target="tpu_custom_call" | custom-call | tf_op jit(solution)/shard_map/losses/pallas_call | solution.py:241
Async XLA Ops:
  0.6 31.5 %collective-permute-start = (bf16[200,768]{1,0:T(8,128)(2,1)}, bf16[200,768]{1,0:T(8,128)(2,1)S(1)}, u32[]{:S(2)}, u32[]{:S(2)}) collective-permute-start(bf16[200,768]{1,0:T(8,128)(2,1)} %param.9), channel_id=1, source_target_pairs={{0,0},{40,8},{16,16},{56,24},{32,32},{8,40},{48,48},{24,56},{72,64... | collective-permute-start | bytes 921608 | tf_op jit(solution)/shard_map/ppermute | solution.py:266
  2.9 0.7 copy-start
  3.6 38.3 %copy-start.1 = (f32[1,768]{1,0:T(1,128)S(1)}, f32[1,768]{1,0:T(1,128)}, u32[]{:S(2)}) copy-start(f32[1,768]{1,0:T(1,128)} %text_ref.1) | copy-start | bytes 9220
  3.6 117.3 %copy-start.2 = (s32[256]{0:T(256)S(1)}, s32[256]{0:T(256)}, u32[]{:S(2)}) copy-start(s32[256]{0:T(256)} %param.12) | copy-start | bytes 3076
  112.7 8.1 %collective-permute-start.1 = (f32[16,16,768]{2,1,0:T(8,128)S(1)}, f32[16,16,768]{2,1,0:T(8,128)S(1)}, u32[]{:S(2)}, u32[]{:S(2)}) collective-permute-start(f32[16,16,768]{2,1,0:T(8,128)S(1)} %all_to_all.23.mine_ref), channel_id=1, source_target_pairs={{0,4},{4,0},{1,5},{5,1},{2,6},{6,2},{3,7},{7,3},{8,12},{12,8},{9,1... | collective-permute-start | bytes 2359304 | tf_op jit(solution)/shard_map/ppermute | solution.py:273

commit v4 on v1

--- a/solution.py
+++ b/solution.py
@@ -15,6 +15,30 @@
 HIGH = lax.Precision.HIGHEST
 F32, BF16 = jnp.float32, jnp.bfloat16
 VMEM_LIMIT = 40 * 1024 * 1024
+GROUP = ("xl", "y", "c")
+
+
+PAIRS = (
+    (3, 6, 1, 4, 0, 2, 5, 7),
+    (5, 0, 4, 3, 7, 1, 6, 2),
+    (0, 7, 3, 6, 1, 4, 2, 5),
+    (4, 5, 2, 1, 6, 3, 7, 0),
+    (1, 4, 7, 2, 5, 0, 3, 6),
+    (6, 3, 0, 5, 2, 7, 4, 1),
+    (2, 1, 6, 7, 4, 5, 0, 3),
+    (7, 2, 5, 0, 3, 6, 1, 4),
+)
+HOPS = (
+    (3, -3, -1, 1, 4, -3, -1, 0),
+    (-3, -1, 2, 0, 3, -4, 0, 3),
+    (0, -2, 1, 3, -3, -1, 4, -2),
+    (4, -4, 0, -2, 2, -2, 1, 1),
+    (1, 3, -3, -1, 1, 3, -3, -1),
+    (-2, 2, -2, 2, -2, 2, -2, 2),
+    (2, 0, 4, -4, 0, 0, 2, -4),
+    (-1, 1, 3, -3, -1, 1, 3, -3),
+)
+MEMBERS = tuple(sum(m << (3 * PAIRS[m][zl]) for m in range(8)) for zl in range(8))
 
 
 def three_terms(value):
@@ -25,13 +49,8 @@
     return first, second, third
 
 
-def pool_kernel(frames_ref, query_ref, tok_hbm, parts_ref, state_ref, tok, spread, mixed, sems):
-    copies = [
-        pltpu.make_async_copy(tok_hbm.at[0, pl.ds(FT * j, FT)], tok.at[pl.ds(FT * j, FT)], sems.at[j])
-        for j in range(FRAMES_HERE)
-    ]
-    for copy in copies:
-        copy.start()
+def pool_kernel(frames_ref, query_ref, tok_ref, parts_ref, state_ref, spread, mixed):
+    tok = tok_ref.at[0]
     spread[...] = jnp.zeros_like(spread)
     rows = query_ref[...].astype(F32)
     for h in range(H):
@@ -40,7 +59,6 @@
     used = frames_ref[0] - lax.axis_index("s") * FRAMES_HERE
     scores = []
     for j in range(FRAMES_HERE):
-        copies[j].wait()
         part = lax.dot_general(
             heads_q, tok[FT * j : FT * (j + 1), :], (((1,), (1,)), ((), ())), preferred_element_type=F32
         )
@@ -56,8 +74,13 @@
         cols = slice(step * n, step * (n + 1))
         out = jnp.dot(terms, tok[:, cols], preferred_element_type=F32)
         mixed[:, cols] = (out[2 * H :] + out[H : 2 * H]) + out[:H]
+    zl = lax.axis_index("zl")
+    members = jnp.int32(0)
+    for place, code in enumerate(MEMBERS):
+        members = jnp.where(zl == place, jnp.int32(code), members)
     for k in range(CHUNKS):
-        parts_ref[k, :, 0:ROWS] = mixed[:, ROWS * k : ROWS * (k + 1)]
+        member = (members >> (3 * (k // 2))) & 7
+        parts_ref[2 * member + k % 2, :, 0:ROWS] = mixed[:, ROWS * k : ROWS * (k + 1)]
     lane = lax.broadcasted_iota(jnp.int32, (H, 128), 1)
     head = lax.broadcasted_iota(jnp.int32, (H, 128), 0)
     row = jnp.where(lane == 64 + head, top, 0.0) + jnp.where(lane == 80 + head, total, 0.0)
@@ -74,14 +97,12 @@
         in_specs=[
             pl.BlockSpec(memory_space=pltpu.SMEM),
             pl.BlockSpec(memory_space=pltpu.VMEM),
-            pl.BlockSpec(memory_space=pl.ANY),
+            pl.BlockSpec(memory_space=pltpu.VMEM),
         ],
         out_specs=(pl.BlockSpec(memory_space=pltpu.VMEM), pl.BlockSpec(memory_space=pltpu.VMEM)),
         scratch_shapes=[
-            pltpu.VMEM((TOK, D), BF16),
             pltpu.VMEM((H, D), F32),
             pltpu.VMEM((H, D), F32),
-            pltpu.SemaphoreType.DMA((FRAMES_HERE,)),
         ],
         compiler_params=pltpu.CompilerParams(vmem_limit_bytes=VMEM_LIMIT),
         cost_estimate=pl.CostEstimate(flops=4 * 64 * TOK * D, bytes_accessed=TOK * D * 2, transcendentals=H * TOK),
@@ -245,9 +266,15 @@
 
 
 def shards(tokens, query, value_weight, frames, text_feat, pair, logit_scale):
+    moves = []
+    for m in range(8):
+        for z in range(32):
+            source = (z + HOPS[m][z % 8]) % 32
+            moves.append(((8 * m + source % 8) * 4 + source // 8, (8 * m + z % 8) * 4 + z // 8))
+    weight = lax.ppermute(value_weight, ("xl", "y", "zl", "s"), moves)
     parts, state = pool(frames, query, tokens)
-    parts = exchange(parts, ("zl", "c"))
-    sums = exchange(project(parts, value_weight), ("zl", "c"))
+    parts = exchange(parts, GROUP)
+    sums = exchange(project(parts, weight), GROUP)
     gathered = exchange(share(sums, state, text_feat), ("s", "zl"))
     block, video_embed = merge(gathered)
     mine = exchange(block, ("xh", "xl", "y"))

time: 134 us -> 119 us (0.89)
  blocking collectives: 113 us -> 79.5 us
  starting transfers between devices: 6.56 us -> 26.8 us
  Pallas kernels: 7.75 us -> 6.06 us
    all_to_all x4, blocking collectives: 113 us -> 79.5 us  [exchange(): return lax.all_to_all(value, axes, 0, 0, tiled=True)]
    ppermute x0 -> x1, starting transfers between devices: none -> 20.6 us  [shards(): weight = lax.ppermute(value_weight, ('xl', 'y', 'zl', 's'), moves)]
    pallas_call x1, Pallas kernels: 3.5 us -> 1.81 us  [pool(): pl.pallas_call(pool_kernel, out_shape=(jax.ShapeDtypeStruct((CHUNKS, H, 2...]
  transfers between devices with their start and end apart: 1 -> 2, of which waited for: 1 -> 1; matrix products, arithmetic and copies ran while one was open for 0% -> 0% of each run, Pallas kernels for 0% -> 2%
where the time goes in v4:
time: 119 us; the launch traced here: 118 us
  blocking collectives  79.5 us (67%)
  starting transfers between devices  26.8 us (23%)
  Pallas kernels  6.06 us (5%)
  local copies, waits for them, and re-layouts  2.62 us (2%)
  between operations  1.97 us (2%)
  waiting for transfers between devices  1.25 us (1%)
    all_to_all x4, blocking collectives, exchange(): return lax.all_to_all(value, axes, 0, 0, tiled=True)  79.5 us
    ppermute x1, starting transfers between devices, shards(): weight = lax.ppermute(value_weight, ('xl', 'y', 'zl', 's'), moves)  20.6 us
    ppermute x1, starting transfers between devices, shards(): other = lax.ppermute(mine, 'c', [(0, 1), (1, 0)])  6.25 us
    unnamed x8, local copies, waits for them, and re-layouts  2.62 us
    pallas_call x1, Pallas kernels, losses(): pl.pallas_call(loss_kernel, out_shape=(jax.ShapeDtypeStruct((1, E), F32),...  2.57 us
  transfers between devices with their start and end apart: 2, of which 1 were waited for; matrix products, arithmetic and copies ran while one was open for 0% of the time, Pallas kernels for 2%

profile of v4, /device:TPU:1, one launch (start us, length us, event | category | flops | bytes accessed | tf_op | source)
XLA Modules:
  0.0 118.3 jit_solution(271941431969426246)
XLA Ops:
  0.6 20.6 %collective-permute-start = (bf16[200,768]{1,0:T(8,128)(2,1)}, bf16[200,768]{1,0:T(8,128)(2,1)S(1)}, u32[]{:S(2)}, u32[]{:S(2)}) collective-permute-start(bf16[200,768]{1,0:T(8,128)(2,1)} %param.9), channel_id=1, source_target_pairs={{24,0},{51,8},{8,16},{32,24},{1,32},{16,40},{40,48},{56,56},{25,1}... | collective-permute-start | bytes 921608 | tf_op jit(solution)/shard_map/ppermute | solution.py:274
  21.8 0.0 copy-start
  21.9 1.9 %copy-done = bf16[1,512,3200]{2,1,0:T(8,128)(2,1)S(1)} copy-done((bf16[1,512,3200]{2,1,0:T(8,128)(2,1)S(1)}, bf16[1,512,3200]{2,1,0:T(8,128)(2,1)}, u32[]{:S(2)}) %copy-start) | copy-done | bytes 3276824
  23.8 0.0 copy-start.1
  23.8 0.7 copy-done.1
  24.5 0.0 copy-start.2
  24.5 0.0 copy-start.3
  24.5 1.8 %pool.1 = (f32[16,16,256]{2,1,0:T(8,128)S(1)}, f32[8,128]{1,0:T(8,128)S(1)}) custom-call(s32[1]{0:T(128)S(6)} %copy.11.frames_ref, bf16[16,200]{1,0:T(8,128)(2,1)S(1)} %copy-done.1, bf16[1,512,3200]{2,1,0:T(8,128)(2,1)S(1)} %copy-done), custom_call_target="tpu_custom_call" | custom-call | flops 419430400 | bytes 3276800 | tf_op jit(solution)/shard_map/pool/pallas_call | solution.py:91
  26.3 12.4 %all_to_all.20.parts_ref = f32[16,16,256]{2,1,0:T(8,128)S(1)} all-to-all(f32[16,16,256]{2,1,0:T(8,128)S(1)} %get-tuple-element.11), channel_id=1, replica_groups=mesh['xh'=2,'xl'=2,'y'=4,'zl'=8,'c'=2,'s'=4] {'xl','y','c'}, dimensions={0} | all-to-all | bytes 524288 | tf_op jit(solution)/shard_map/all_to_all | solution.py:265
  38.7 0.0 collective-permute-done.weight_ref
  38.7 0.5 project.1
  39.2 9.3 %all_to_all.21.sums_ref = f32[16,8,128]{2,1,0:T(8,128)S(1)} all-to-all(f32[16,8,128]{2,1,0:T(8,128)S(1)} %project.1), channel_id=1, replica_groups=mesh['xh'=2,'xl'=2,'y'=4,'zl'=8,'c'=2,'s'=4] {'xl','y','c'}, dimensions={0} | all-to-all | bytes 131072 | tf_op jit(solution)/shard_map/all_to_all | solution.py:265
  48.5 0.0 copy-done.2
  48.5 0.1 share.1
  48.6 42.8 %all_to_all.22.parts_ref = f32[32,8,128]{2,1,0:T(8,128)S(1)} all-to-all(f32[32,8,128]{2,1,0:T(8,128)S(1)} %share.1), channel_id=1, replica_groups=mesh['xh'=2,'xl'=2,'y'=4,'zl'=8,'c'=2,'s'=4] {'s','zl'}, dimensions={0} | all-to-all | bytes 262144 | tf_op jit(solution)/shard_map/all_to_all | solution.py:265
  91.4 1.1 merge.1
  92.5 15.1 %all_to_all.23.mine_ref = f32[16,16,768]{2,1,0:T(8,128)S(1)} all-to-all(f32[16,16,768]{2,1,0:T(8,128)S(1)} %get-tuple-element.14), channel_id=1, replica_groups=mesh['xh'=2,'xl'=2,'y'=4,'zl'=8,'c'=2,'s'=4] {'xh','xl','y'}, dimensions={0} | all-to-all | bytes 1572864 | tf_op jit(solution)/shard_map/all_to_all | solution.py:265
  107.5 6.2 %collective-permute-start.1 = (f32[16,16,768]{2,1,0:T(8,128)S(1)}, f32[16,16,768]{2,1,0:T(8,128)S(1)}, u32[]{:S(2)}, u32[]{:S(2)}) collective-permute-start(f32[16,16,768]{2,1,0:T(8,128)S(1)} %all_to_all.23.mine_ref), channel_id=1, source_target_pairs={{0,4},{4,0},{1,5},{5,1},{2,6},{6,2},{3,7},{7,3},{8,12},{12,8},{9,1... | collective-permute-start | bytes 2359304 | tf_op jit(solution)/shard_map/ppermute | solution.py:281
  114.4 1.2 %collective-permute-done.1.other_ref = f32[16,16,768]{2,1,0:T(8,128)S(1)} collective-permute-done((f32[16,16,768]{2,1,0:T(8,128)S(1)}, f32[16,16,768]{2,1,0:T(8,128)S(1)}, u32[]{:S(2)}, u32[]{:S(2)}) %collective-permute-start.1) | collective-permute-done | bytes 786464 | tf_op jit(solution)/shard_map/ppermute | solution.py:281
  115.7 0.0 copy-done.3
  115.7 2.6 %losses.1 = (f32[1,768]{1,0:T(1,128)}, f32[1,768]{1,0:T(1,128)}, f32[1,1]{1,0:T(1,128)}) custom-call(f32[1]{0:T(128)} %bitcast.3.scale_ref, s32[1,256]{1,0:T(1,128)S(1)} %bitcast.4, f32[16,16,768]{2,1,0:T(8,128)S(1)} %all_to_all.23.mine_ref, f32[16,16,768]{2,1,0:T(8,128)S(1)} %collective-permute-done.1.other_ref), custom_call_target="tpu_custom_call" | custom-call | tf_op jit(solution)/shard_map/losses/pallas_call | solution.py:249
Async XLA Ops:
  0.6 38.1 %collective-permute-start = (bf16[200,768]{1,0:T(8,128)(2,1)}, bf16[200,768]{1,0:T(8,128)(2,1)S(1)}, u32[]{:S(2)}, u32[]{:S(2)}) collective-permute-start(bf16[200,768]{1,0:T(8,128)(2,1)} %param.9), channel_id=1, source_target_pairs={{24,0},{51,8},{8,16},{32,24},{1,32},{16,40},{40,48},{56,56},{25,1}... | collective-permute-start | bytes 921608 | tf_op jit(solution)/shard_map/ppermute | solution.py:274
  21.8 1.9 %copy-start = (bf16[1,512,3200]{2,1,0:T(8,128)(2,1)S(1)}, bf16[1,512,3200]{2,1,0:T(8,128)(2,1)}, u32[]{:S(2)}) copy-start(bf16[1,512,3200]{2,1,0:T(8,128)(2,1)} %tok_ref.1) | copy-start | bytes 9830404
  23.8 0.7 copy-start.1
  24.5 24.0 %copy-start.2 = (f32[1,768]{1,0:T(1,128)S(1)}, f32[1,768]{1,0:T(1,128)}, u32[]{:S(2)}) copy-start(f32[1,768]{1,0:T(1,128)} %text_ref.1) | copy-start | bytes 9220
  24.5 91.2 %copy-start.3 = (s32[256]{0:T(256)S(1)}, s32[256]{0:T(256)}, u32[]{:S(2)}) copy-start(s32[256]{0:T(256)} %param.12) | copy-start | bytes 3076
  107.5 8.1 %collective-permute-start.1 = (f32[16,16,768]{2,1,0:T(8,128)S(1)}, f32[16,16,768]{2,1,0:T(8,128)S(1)}, u32[]{:S(2)}, u32[]{:S(2)}) collective-permute-start(f32[16,16,768]{2,1,0:T(8,128)S(1)} %all_to_all.23.mine_ref), channel_id=1, source_target_pairs={{0,4},{4,0},{1,5},{5,1},{2,6},{6,2},{3,7},{7,3},{8,12},{12,8},{9,1... | collective-permute-start | bytes 2359304 | tf_op jit(solution)/shard_map/ppermute | solution.py:281

commit v5 on v4

--- a/solution.py
+++ b/solution.py
@@ -49,13 +49,30 @@
     return first, second, third
 
 
-def pool_kernel(frames_ref, query_ref, tok_ref, parts_ref, state_ref, spread, mixed):
-    tok = tok_ref.at[0]
+def spread_kernel(query_ref, out_ref, spread):
     spread[...] = jnp.zeros_like(spread)
     rows = query_ref[...].astype(F32)
     for h in range(H):
         spread[h : h + 1, W_H * h : W_H * (h + 1)] = rows[h : h + 1, :]
-    heads_q = spread[...].astype(BF16)
+    out_ref[...] = spread[...].astype(BF16)
+
+
+def spread_heads(query):
+    return pl.pallas_call(
+        spread_kernel,
+        out_shape=jax.ShapeDtypeStruct((H, D), BF16),
+        in_specs=[pl.BlockSpec(memory_space=pltpu.VMEM)],
+        out_specs=pl.BlockSpec(memory_space=pltpu.VMEM),
+        scratch_shapes=[pltpu.VMEM((H, D), F32)],
+        compiler_params=pltpu.CompilerParams(vmem_limit_bytes=VMEM_LIMIT),
+        cost_estimate=pl.CostEstimate(flops=10**9, bytes_accessed=10**7, transcendentals=0),
+        name="spread_heads",
+    )(query)
+
+
+def pool_kernel(frames_ref, query_ref, tok_ref, parts_ref, state_ref, mixed):
+    tok = tok_ref.at[0]
+    heads_q = query_ref[...]
     used = frames_ref[0] - lax.axis_index("s") * FRAMES_HERE
     scores = []
     for j in range(FRAMES_HERE):
@@ -74,7 +91,7 @@
         cols = slice(step * n, step * (n + 1))
         out = jnp.dot(terms, tok[:, cols], preferred_element_type=F32)
         mixed[:, cols] = (out[2 * H :] + out[H : 2 * H]) + out[:H]
-    zl = lax.axis_index("zl")
+    zl = lax.axis_index("zab") * 2 + lax.axis_index("zc")
     members = jnp.int32(0)
     for place, code in enumerate(MEMBERS):
         members = jnp.where(zl == place, jnp.int32(code), members)
@@ -100,10 +117,7 @@
             pl.BlockSpec(memory_space=pltpu.VMEM),
         ],
         out_specs=(pl.BlockSpec(memory_space=pltpu.VMEM), pl.BlockSpec(memory_space=pltpu.VMEM)),
-        scratch_shapes=[
-            pltpu.VMEM((H, D), F32),
-            pltpu.VMEM((H, D), F32),
-        ],
+        scratch_shapes=[pltpu.VMEM((H, D), F32)],
         compiler_params=pltpu.CompilerParams(vmem_limit_bytes=VMEM_LIMIT),
         cost_estimate=pl.CostEstimate(flops=4 * 64 * TOK * D, bytes_accessed=TOK * D * 2, transcendentals=H * TOK),
         name="pool",
@@ -160,7 +174,7 @@
 def share(sums, state, text):
     return pl.pallas_call(
         share_kernel,
-        out_shape=jax.ShapeDtypeStruct((32, 8, 128), F32),
+        out_shape=jax.ShapeDtypeStruct((16, 8, 128), F32),
         in_specs=[pl.BlockSpec(memory_space=pltpu.VMEM)] * 3,
         out_specs=pl.BlockSpec(memory_space=pltpu.VMEM),
         compiler_params=pltpu.CompilerParams(vmem_limit_bytes=VMEM_LIMIT),
@@ -173,35 +187,35 @@
 
 
 def merge_kernel(parts_ref, out_ref, video_ref, rows):
-    ends = [parts_ref[8 * s : 8 * (s + 1), 7, :] for s in range(4)]
+    ends = [parts_ref[4 * s : 4 * (s + 1), 7, :] for s in range(4)]
     tops = [end[:, 64 : 64 + H] for end in ends]
     totals = [end[:, 80 : 80 + H] for end in ends]
     top = jnp.maximum(jnp.maximum(tops[0], tops[1]), jnp.maximum(tops[2], tops[3]))
     scales = [jnp.exp(t - top) for t in tops]
     total = sum(scale * value for scale, value in zip(scales, totals))
-    scales = jnp.concatenate([scale / total for scale in scales], axis=0)
     lane = lax.broadcasted_iota(jnp.int32, (H, E), 1) // W_E
     head = lax.broadcasted_iota(jnp.int32, (H, E), 0)
     spread = jnp.where(lane == head, F32(1.0), F32(0.0))
-    factors = jnp.dot(scales, spread, precision=HIGH, preferred_element_type=F32)
-    pooled = jnp.zeros((8, E), F32)
+    factors = jnp.concatenate([scale / total for scale in scales], axis=0)
+    factors = jnp.dot(factors, spread, precision=HIGH, preferred_element_type=F32)
+    pooled = jnp.zeros((4, E), F32)
     texts = []
     for s in range(4):
-        mine = [parts_ref[8 * s : 8 * (s + 1), r, :] for r in range(6)]
-        pooled = pooled + factors[8 * s : 8 * (s + 1)] * jnp.concatenate(mine, axis=1)
-        texts += [parts_ref[8 * s : 8 * (s + 1), 6, :], ends[s][:, 0:64]]
+        mine = [parts_ref[4 * s : 4 * (s + 1), r, :] for r in range(6)]
+        pooled = pooled + factors[4 * s : 4 * (s + 1)] * jnp.concatenate(mine, axis=1)
+        texts += [parts_ref[4 * s : 4 * (s + 1), 6, :], ends[s][:, 0:64]]
     videos = unit_rows(pooled)
     texts = unit_rows(jnp.concatenate(texts, axis=1))
-    out_ref[:, 0:8, :] = jnp.broadcast_to(videos[None], (16, 8, E))
-    out_ref[:, 8:16, :] = jnp.broadcast_to(texts[None], (16, 8, E))
-    rows[...] = videos
-    video_ref[...] = rows[pl.ds(lax.axis_index("zl"), 1), :]
+    rows[0:4, :] = videos
+    rows[4:8, :] = texts
+    out_ref[...] = jnp.broadcast_to(rows[...][None], (32, 8, E)).reshape(256, E)
+    video_ref[...] = rows[pl.ds(lax.axis_index("zab"), 1), :]
 
 
 def merge(parts):
     return pl.pallas_call(
         merge_kernel,
-        out_shape=(jax.ShapeDtypeStruct((16, 16, E), F32), jax.ShapeDtypeStruct((1, E), F32)),
+        out_shape=(jax.ShapeDtypeStruct((256, E), F32), jax.ShapeDtypeStruct((1, E), F32)),
         in_specs=[pl.BlockSpec(memory_space=pltpu.VMEM)],
         out_specs=(pl.BlockSpec(memory_space=pltpu.VMEM), pl.BlockSpec(memory_space=pltpu.VMEM)),
         scratch_shapes=[pltpu.VMEM((8, E), F32)],
@@ -210,15 +224,22 @@
     )(parts)
 
 
+def clip_of(row):
+    return (row % 128 // 8) * 16 + (row % 4) * 4 + (row // 4 % 2) * 2 + row // 128
+
+
 def loss_kernel(scale_ref, pair_ref, mine_ref, other_ref, video_ref, text_ref, loss_ref, videos, texts, grads):
     core = lax.axis_index("c")
     here = lax.axis_index("xh") * 2 + lax.axis_index("xl")
-    place = (here * 4 + lax.axis_index("y")) * 8 + lax.axis_index("zl")
+    place = ((here * 4 + lax.axis_index("y")) * 2 + lax.axis_index("zc")) * 4 + lax.axis_index("zab")
     n = 256
     for ref, start in ((mine_ref, core * 128), (other_ref, (1 - core) * 128)):
         start = pl.multiple_of(start, 128)
-        videos[pl.ds(start, 128), :] = ref[:, 0:8, :].reshape(128, E)
-        texts[pl.ds(start, 128), :] = ref[:, 8:16, :].reshape(128, E)
+        blocks = ref[...].reshape(16, 2, 8, E)
+        even, odd = blocks[:, 0], blocks[:, 1]
+        low = lax.broadcasted_iota(jnp.int32, (16, 8, E), 1) < 4
+        videos[pl.ds(start, 128), :] = jnp.where(low, even, pltpu.roll(odd, 4, 1)).reshape(128, E)
+        texts[pl.ds(start, 128), :] = jnp.where(low, pltpu.roll(even, 4, 1), odd).reshape(128, E)
     v, t = videos[...], texts[...]
     scale = scale_ref[0]
     logits = scale * lax.dot_general(
@@ -229,8 +250,7 @@
     col_sum = jnp.sum(expd, axis=0, keepdims=True)
     row = lax.broadcasted_iota(jnp.int32, (n, n), 0)
     col = lax.broadcasted_iota(jnp.int32, (n, n), 1)
-    row_id = 2 * (row % 128) + row // 128
-    col_id = 2 * (col % 128) + col // 128
+    row_id, col_id = clip_of(row), clip_of(col)
     pairs = jnp.sum(jnp.where(col == row_id, pair_ref[...].astype(F32), 0.0), axis=1, keepdims=True)
     hot = pairs == col_id.astype(F32)
     positive = jnp.sum(jnp.where(hot, logits, 0.0))
@@ -271,29 +291,31 @@
         for z in range(32):
             source = (z + HOPS[m][z % 8]) % 32
             moves.append(((8 * m + source % 8) * 4 + source // 8, (8 * m + z % 8) * 4 + z // 8))
-    weight = lax.ppermute(value_weight, ("xl", "y", "zl", "s"), moves)
-    parts, state = pool(frames, query, tokens)
+    heads_q = spread_heads(query)
+    value_weight, heads_q = lax.optimization_barrier((value_weight, heads_q))
+    weight = lax.ppermute(value_weight, ("xl", "y", "zab", "zc", "s"), moves)
+    parts, state = pool(frames, heads_q, tokens)
     parts = exchange(parts, GROUP)
     sums = exchange(project(parts, weight), GROUP)
-    gathered = exchange(share(sums, state, text_feat), ("s", "zl"))
+    gathered = exchange(share(sums, state, text_feat), ("s", "zab"))
     block, video_embed = merge(gathered)
-    mine = exchange(block, ("xh", "xl", "y"))
+    mine = exchange(block, ("xh", "xl", "y", "zc"))
     other = lax.ppermute(mine, "c", [(0, 1), (1, 0)])
     grad_video, grad_text, loss = losses(logit_scale.reshape(1), pair.reshape(1, -1), mine, other)
     return (video_embed, grad_video, grad_text, loss.reshape(()))
 
 
 def solution(mesh):
-    axes = ("xh", "xl", "y", "zl", "c", "s")
-    fine = Mesh(mesh.devices.reshape(2, 2, 4, 8, 2, 4), axes)
-    clips = axes[:5]
+    axes = ("xh", "xl", "y", "zab", "zc", "c", "s")
+    fine = Mesh(mesh.devices.reshape(2, 2, 4, 4, 2, 2, 4), axes)
+    clips = axes[:6]
     return jax.shard_map(
         shards,
         mesh=fine,
         in_specs=(
             P(clips, "s", None),
             P(),
-            P(("zl", "c"), None),
+            P(("zab", "zc", "c"), None),
             P(clips),
             P(clips, None),
             P(),

time: 119 us -> 111 us (0.933)
  blocking collectives: 79.5 us -> 73 us
    all_to_all x4, blocking collectives: 79.5 us -> 73 us  [exchange(): return lax.all_to_all(value, axes, 0, 0, tiled=True)]
    unnamed x8 -> x10, local copies, waits for them, and re-layouts: 2.62 us -> 1.87 us
where the time goes in v5:
time: 111 us; the launch traced here: 110 us
  blocking collectives  73 us (66%)
  starting transfers between devices  26 us (23%)
  Pallas kernels  6.13 us (6%)
  between operations  2 us (2%)
  local copies, waits for them, and re-layouts  1.87 us (2%)
  waiting for transfers between devices  1.25 us (1%)
    all_to_all x4, blocking collectives, exchange(): return lax.all_to_all(value, axes, 0, 0, tiled=True)  73 us
    ppermute x1, starting transfers between devices, shards(): weight = lax.ppermute(value_weight, ('xl', 'y', 'zab', 'zc', 's'), moves)  20.5 us
    ppermute x1, starting transfers between devices, shards(): other = lax.ppermute(mine, 'c', [(0, 1), (1, 0)])  5.44 us
    pallas_call x1, Pallas kernels, losses(): pl.pallas_call(loss_kernel, out_shape=(jax.ShapeDtypeStruct((1, E), F32),...  2.61 us
  transfers between devices with their start and end apart: 2, of which 1 were waited for; matrix products, arithmetic and copies ran while one was open for 0% of the time, Pallas kernels for 2%

profile of v5, /device:TPU:1, one launch (start us, length us, event | category | flops | bytes accessed | tf_op | source)
XLA Modules:
  0.0 110.2 jit_solution(4097713886197881730)
XLA Ops:
  0.6 0.0 copy-start
  0.6 0.0 copy-start.1
  0.7 0.0 copy-start.3
  0.7 0.8 copy-done.3
  1.5 0.0 copy-start.4
  1.5 0.1 spread_heads.1.query_ref
  1.6 1.0 copy-done.4
  2.6 20.5 %collective-permute-start = (bf16[200,768]{1,0:T(8,128)(2,1)S(1)}, bf16[200,768]{1,0:T(8,128)(2,1)S(1)}, u32[]{:S(2)}, u32[]{:S(2)}) collective-permute-start(bf16[200,768]{1,0:T(8,128)(2,1)S(1)} %copy-done.4), channel_id=1, source_target_pairs={{24,0},{51,8},{8,16},{32,24},{1,32},{16,40},{40,48},{56,56},{25,1}... | collective-permute-start | bytes 921608 | tf_op jit(solution)/shard_map/ppermute | solution.py:296
  23.8 0.0 copy-done
  23.8 0.0 copy-start.2
  23.8 1.8 %pool.1 = (f32[16,16,256]{2,1,0:T(8,128)S(1)}, f32[8,128]{1,0:T(8,128)S(1)}) custom-call(s32[1]{0:T(128)S(6)} %copy.11.frames_ref, bf16[16,3200]{1,0:T(8,128)(2,1)S(1)} %spread_heads.1.query_ref, bf16[1,512,3200]{2,1,0:T(8,128)(2,1)S(1)} %copy-done), custom_call_target="tpu_custom_call" | custom-call | flops 419430400 | bytes 3276800 | tf_op jit(solution)/shard_map/pool/pallas_call | solution.py:108
  25.6 12.4 %all_to_all.26.parts_ref = f32[16,16,256]{2,1,0:T(8,128)S(1)} all-to-all(f32[16,16,256]{2,1,0:T(8,128)S(1)} %get-tuple-element.14), channel_id=1, replica_groups=mesh['xh'=2,'xl'=2,'y'=4,'zab'=4,'zc'=2,'c'=2,'s'=4] {'xl','y','c'}, dimensions={0} | all-to-all | bytes 524288 | tf_op jit(solution)/shard_map/all_to_all | solution.py:285
  38.0 0.0 collective-permute-done.weight_ref
  38.0 0.5 project.1
  38.6 9.3 %all_to_all.27.sums_ref = f32[16,8,128]{2,1,0:T(8,128)S(1)} all-to-all(f32[16,8,128]{2,1,0:T(8,128)S(1)} %project.1), channel_id=1, replica_groups=mesh['xh'=2,'xl'=2,'y'=4,'zab'=4,'zc'=2,'c'=2,'s'=4] {'xl','y','c'}, dimensions={0} | all-to-all | bytes 131072 | tf_op jit(solution)/shard_map/all_to_all | solution.py:285
  47.8 0.0 copy-done.1
  47.8 0.1 share.1
  47.9 34.2 %all_to_all.28.parts_ref = f32[16,8,128]{2,1,0:T(8,128)S(1)} all-to-all(f32[16,8,128]{2,1,0:T(8,128)S(1)} %share.1), channel_id=1, replica_groups=mesh['xh'=2,'xl'=2,'y'=4,'zab'=4,'zc'=2,'c'=2,'s'=4] {'s','zab'}, dimensions={0} | all-to-all | bytes 131072 | tf_op jit(solution)/shard_map/all_to_all | solution.py:285
  82.2 1.1 merge.1
  83.2 17.0 %all_to_all.29 = f32[32,8,768]{2,1,0:T(8,128)S(1)} all-to-all(f32[32,8,768]{2,1,0:T(8,128)S(1)} %bitcast.8), channel_id=1, replica_groups=mesh['xh'=2,'xl'=2,'y'=4,'zab'=4,'zc'=2,'c'=2,'s'=4] {'xh','xl','y','zc'}, dimensions={0} | all-to-all | bytes 1572864 | tf_op jit(solution)/shard_map/all_to_all | solution.py:285
  100.2 5.4 %collective-permute-start.1 = (f32[256,768]{1,0:T(8,128)S(1)}, f32[256,768]{1,0:T(8,128)S(1)}, u32[]{:S(2)}, u32[]{:S(2)}) collective-permute-start(f32[256,768]{1,0:T(8,128)S(1)} %bitcast.6), channel_id=1, source_target_pairs={{0,4},{4,0},{1,5},{5,1},{2,6},{6,2},{3,7},{7,3},{8,12},{12,8},{9,1... | collective-permute-start | bytes 2359304 | tf_op jit(solution)/shard_map/ppermute | solution.py:303
  106.3 1.2 %collective-permute-done.1.other_ref = f32[256,768]{1,0:T(8,128)S(1)} collective-permute-done((f32[256,768]{1,0:T(8,128)S(1)}, f32[256,768]{1,0:T(8,128)S(1)}, u32[]{:S(2)}, u32[]{:S(2)}) %collective-permute-start.1) | collective-permute-done | bytes 786464 | tf_op jit(solution)/shard_map/ppermute | solution.py:303
  107.6 0.0 copy-done.2
  107.6 2.6 %losses.1 = (f32[1,768]{1,0:T(1,128)}, f32[1,768]{1,0:T(1,128)}, f32[1,1]{1,0:T(1,128)}) custom-call(f32[1]{0:T(128)} %bitcast.5.scale_ref, s32[1,256]{1,0:T(1,128)S(1)} %bitcast.9, f32[256,768]{1,0:T(8,128)S(1)} %bitcast.7, f32[256,768]{1,0:T(8,128)S(1)} %collective-permute-done.1.other_ref), custom_call_target="tpu_custom_call" | custom-call | tf_op jit(solution)/shard_map/losses/pallas_call | solution.py:269
Async XLA Ops:
  0.6 23.2 %copy-start = (bf16[1,512,3200]{2,1,0:T(8,128)(2,1)S(1)}, bf16[1,512,3200]{2,1,0:T(8,128)(2,1)}, u32[]{:S(2)}) copy-start(bf16[1,512,3200]{2,1,0:T(8,128)(2,1)} %tok_ref.1) | copy-start | bytes 9830404
  0.6 47.2 %copy-start.1 = (f32[1,768]{1,0:T(1,128)S(1)}, f32[1,768]{1,0:T(1,128)}, u32[]{:S(2)}) copy-start(f32[1,768]{1,0:T(1,128)} %text_ref.1) | copy-start | bytes 9220
  0.7 0.8 copy-start.3
  1.5 1.1 %copy-start.4 = (bf16[200,768]{1,0:T(8,128)(2,1)S(1)}, bf16[200,768]{1,0:T(8,128)(2,1)}, u32[]{:S(2)}) copy-start(bf16[200,768]{1,0:T(8,128)(2,1)} %param.9) | copy-start | bytes 921604
  2.6 35.4 %collective-permute-start = (bf16[200,768]{1,0:T(8,128)(2,1)S(1)}, bf16[200,768]{1,0:T(8,128)(2,1)S(1)}, u32[]{:S(2)}, u32[]{:S(2)}) collective-permute-start(bf16[200,768]{1,0:T(8,128)(2,1)S(1)} %copy-done.4), channel_id=1, source_target_pairs={{24,0},{51,8},{8,16},{32,24},{1,32},{16,40},{40,48},{56,56},{25,1}... | collective-permute-start | bytes 921608 | tf_op jit(solution)/shard_map/ppermute | solution.py:296
  23.8 83.8 %copy-start.2 = (s32[256]{0:T(256)S(1)}, s32[256]{0:T(256)}, u32[]{:S(2)}) copy-start(s32[256]{0:T(256)} %param.12) | copy-start | bytes 3076
  100.2 7.3 %collective-permute-start.1 = (f32[256,768]{1,0:T(8,128)S(1)}, f32[256,768]{1,0:T(8,128)S(1)}, u32[]{:S(2)}, u32[]{:S(2)}) collective-permute-start(f32[256,768]{1,0:T(8,128)S(1)} %bitcast.6), channel_id=1, source_target_pairs={{0,4},{4,0},{1,5},{5,1},{2,6},{6,2},{3,7},{7,3},{8,12},{12,8},{9,1... | collective-permute-start | bytes 2359304 | tf_op jit(solution)/shard_map/ppermute | solution.py:303

commit v6 on v5

--- a/solution.py
+++ b/solution.py
@@ -49,31 +49,30 @@
     return first, second, third
 
 
-def spread_kernel(query_ref, out_ref, spread):
+def used_kernel(frames_ref, out_ref):
+    out_ref[...] = jnp.full((8, 128), frames_ref[0] - lax.axis_index("s") * FRAMES_HERE, jnp.int32)
+
+
+def used_frames(frames):
+    return pl.pallas_call(
+        used_kernel,
+        out_shape=jax.ShapeDtypeStruct((8, 128), jnp.int32),
+        in_specs=[pl.BlockSpec(memory_space=pltpu.SMEM)],
+        out_specs=pl.BlockSpec(memory_space=pltpu.VMEM),
+        compiler_params=pltpu.CompilerParams(vmem_limit_bytes=1024 * 1024),
+        cost_estimate=pl.CostEstimate(flops=10**9, bytes_accessed=10**7, transcendentals=0),
+        name="used_frames",
+    )(frames)
+
+
+def pool_kernel(used_ref, query_ref, tok_ref, parts_ref, state_ref, spread, mixed):
+    tok = tok_ref.at[0]
     spread[...] = jnp.zeros_like(spread)
     rows = query_ref[...].astype(F32)
     for h in range(H):
         spread[h : h + 1, W_H * h : W_H * (h + 1)] = rows[h : h + 1, :]
-    out_ref[...] = spread[...].astype(BF16)
-
-
-def spread_heads(query):
-    return pl.pallas_call(
-        spread_kernel,
-        out_shape=jax.ShapeDtypeStruct((H, D), BF16),
-        in_specs=[pl.BlockSpec(memory_space=pltpu.VMEM)],
-        out_specs=pl.BlockSpec(memory_space=pltpu.VMEM),
-        scratch_shapes=[pltpu.VMEM((H, D), F32)],
-        compiler_params=pltpu.CompilerParams(vmem_limit_bytes=VMEM_LIMIT),
-        cost_estimate=pl.CostEstimate(flops=10**9, bytes_accessed=10**7, transcendentals=0),
-        name="spread_heads",
-    )(query)
-
-
-def pool_kernel(frames_ref, query_ref, tok_ref, parts_ref, state_ref, mixed):
-    tok = tok_ref.at[0]
-    heads_q = query_ref[...]
-    used = frames_ref[0] - lax.axis_index("s") * FRAMES_HERE
+    heads_q = spread[...].astype(BF16)
+    used = used_ref[0:1, 0:1]
     scores = []
     for j in range(FRAMES_HERE):
         part = lax.dot_general(
@@ -104,7 +103,7 @@
     state_ref[...] = jnp.broadcast_to(jnp.sum(row, axis=0, keepdims=True), (8, 128))
 
 
-def pool(frames, query, tokens):
+def pool(used, query, tokens):
     return pl.pallas_call(
         pool_kernel,
         out_shape=(
@@ -112,16 +111,16 @@
             jax.ShapeDtypeStruct((8, 128), F32),
         ),
         in_specs=[
-            pl.BlockSpec(memory_space=pltpu.SMEM),
+            pl.BlockSpec(memory_space=pltpu.VMEM),
             pl.BlockSpec(memory_space=pltpu.VMEM),
             pl.BlockSpec(memory_space=pltpu.VMEM),
         ],
         out_specs=(pl.BlockSpec(memory_space=pltpu.VMEM), pl.BlockSpec(memory_space=pltpu.VMEM)),
-        scratch_shapes=[pltpu.VMEM((H, D), F32)],
+        scratch_shapes=[pltpu.VMEM((H, D), F32), pltpu.VMEM((H, D), F32)],
         compiler_params=pltpu.CompilerParams(vmem_limit_bytes=VMEM_LIMIT),
         cost_estimate=pl.CostEstimate(flops=4 * 64 * TOK * D, bytes_accessed=TOK * D * 2, transcendentals=H * TOK),
         name="pool",
-    )(frames, query, tokens)
+    )(used, query, tokens)
 
 
 def project_kernel(parts_ref, weight_ref, out_ref):
@@ -195,9 +194,10 @@
     total = sum(scale * value for scale, value in zip(scales, totals))
     lane = lax.broadcasted_iota(jnp.int32, (H, E), 1) // W_E
     head = lax.broadcasted_iota(jnp.int32, (H, E), 0)
-    spread = jnp.where(lane == head, F32(1.0), F32(0.0))
-    factors = jnp.concatenate([scale / total for scale in scales], axis=0)
-    factors = jnp.dot(factors, spread, precision=HIGH, preferred_element_type=F32)
+    spread = jnp.where(lane == head, F32(1.0), F32(0.0)).astype(BF16)
+    terms = three_terms(jnp.concatenate([scale / total for scale in scales], axis=0))
+    terms = jnp.dot(jnp.concatenate(terms, axis=0), spread, preferred_element_type=F32)
+    factors = (terms[32:48] + terms[16:32]) + terms[0:16]
     pooled = jnp.zeros((4, E), F32)
     texts = []
     for s in range(4):
@@ -258,8 +258,8 @@
     grad = (expd / row_sum + expd / col_sum - jnp.where(hot, F32(2.0), F32(0.0))) / (2.0 * n)
     grads[...] = grad
     own = core * 128 + place
-    own_row = jnp.broadcast_to(grads[pl.ds(own, 1), :], (8, n))
-    video_ref[...] = scale * jnp.dot(own_row, t, precision=HIGH, preferred_element_type=F32)[0:1, :]
+    own_row = jnp.sum(jnp.where(row == col, grads[pl.ds(own, 1), :], 0.0), axis=1, keepdims=True)
+    video_ref[...] = scale * jnp.sum(own_row * t, axis=0, keepdims=True)
     own_col = jnp.sum(jnp.where(col == own, grad, 0.0), axis=1, keepdims=True)
     text_ref[...] = scale * jnp.sum(own_col * v, axis=0, keepdims=True)
 
@@ -291,10 +291,10 @@
         for z in range(32):
             source = (z + HOPS[m][z % 8]) % 32
             moves.append(((8 * m + source % 8) * 4 + source // 8, (8 * m + z % 8) * 4 + z // 8))
-    heads_q = spread_heads(query)
-    value_weight, heads_q = lax.optimization_barrier((value_weight, heads_q))
+    used = used_frames(frames)
+    value_weight, used = lax.optimization_barrier((value_weight, used))
     weight = lax.ppermute(value_weight, ("xl", "y", "zab", "zc", "s"), moves)
-    parts, state = pool(frames, heads_q, tokens)
+    parts, state = pool(used, query, tokens)
     parts = exchange(parts, GROUP)
     sums = exchange(project(parts, weight), GROUP)
     gathered = exchange(share(sums, state, text_feat), ("s", "zab"))

time: 111 us -> 108 us (0.973)
  local copies, waits for them, and re-layouts: 1.87 us -> 0.13 us
    unnamed x10, local copies, waits for them, and re-layouts: 1.87 us -> 0.13 us
where the time goes in v6:
time: 108 us
  blocking collectives  73 us (68%)
  starting transfers between devices  26.1 us (24%)
  Pallas kernels  5.55 us (5%)
  between operations  2.17 us (2%)
  waiting for transfers between devices  1.25 us (1%)
    all_to_all x4, blocking collectives, exchange(): return lax.all_to_all(value, axes, 0, 0, tiled=True)  73 us
    ppermute x1, starting transfers between devices, shards(): weight = lax.ppermute(value_weight, ('xl', 'y', 'zab', 'zc', 's'), moves)  20.7 us
    ppermute x1, starting transfers between devices, shards(): other = lax.ppermute(mine, 'c', [(0, 1), (1, 0)])  5.45 us
  transfers between devices with their start and end apart: 2, of which 1 were waited for; matrix products, arithmetic and copies ran while one was open for 0% of the time, Pallas kernels for 2%

profile of v6, /device:TPU:1, one launch (start us, length us, event | category | flops | bytes accessed | tf_op | source)
XLA Modules:
  0.0 108.2 jit_solution(1697464642499224827)
XLA Ops:
  0.6 0.0 copy-start.4
  0.6 0.0 copy-start
  0.7 0.0 copy-start.1
  1.5 0.0 copy-start.2
  1.5 0.1 copy-done.4
  1.6 0.0 copy-start.3
  1.6 20.7 %collective-permute-start = (bf16[200,768]{1,0:T(8,128)(2,1)S(1)}, bf16[200,768]{1,0:T(8,128)(2,1)S(1)}, u32[]{:S(2)}, u32[]{:S(2)}) collective-permute-start(bf16[200,768]{1,0:T(8,128)(2,1)S(1)} %copy-done.4), channel_id=1, source_target_pairs={{24,0},{51,8},{8,16},{32,24},{1,32},{16,40},{40,48},{56,56},{25,1}... | collective-permute-start | bytes 921608 | tf_op jit(solution)/shard_map/ppermute | solution.py:296
  22.3 0.0 copy-done
  22.3 0.0 copy-done.1
  22.3 1.8 %pool.1 = (f32[16,16,256]{2,1,0:T(8,128)S(1)}, f32[8,128]{1,0:T(8,128)S(1)}) custom-call(s32[8,128]{1,0:T(8,128)S(1)} %used_frames.1.used_ref, bf16[16,200]{1,0:T(8,128)(2,1)S(1)} %copy-done.1, bf16[1,512,3200]{2,1,0:T(8,128)(2,1)S(1)} %copy-done), custom_call_target="tpu_custom_call" | custom-call | flops 419430400 | bytes 3276800 | tf_op jit(solution)/shard_map/pool/pallas_call | solution.py:107
  24.1 12.4 %all_to_all.26.parts_ref = f32[16,16,256]{2,1,0:T(8,128)S(1)} all-to-all(f32[16,16,256]{2,1,0:T(8,128)S(1)} %get-tuple-element.14), channel_id=1, replica_groups=mesh['xh'=2,'xl'=2,'y'=4,'zab'=4,'zc'=2,'c'=2,'s'=4] {'xl','y','c'}, dimensions={0} | all-to-all | bytes 524288 | tf_op jit(solution)/shard_map/all_to_all | solution.py:285
  36.6 0.0 collective-permute-done.weight_ref
  36.6 0.5 project.1
  37.1 9.3 %all_to_all.27.sums_ref = f32[16,8,128]{2,1,0:T(8,128)S(1)} all-to-all(f32[16,8,128]{2,1,0:T(8,128)S(1)} %project.1), channel_id=1, replica_groups=mesh['xh'=2,'xl'=2,'y'=4,'zab'=4,'zc'=2,'c'=2,'s'=4] {'xl','y','c'}, dimensions={0} | all-to-all | bytes 131072 | tf_op jit(solution)/shard_map/all_to_all | solution.py:285
  46.4 0.0 copy-done.2
  46.4 0.1 share.1
  46.5 34.2 %all_to_all.28.parts_ref = f32[16,8,128]{2,1,0:T(8,128)S(1)} all-to-all(f32[16,8,128]{2,1,0:T(8,128)S(1)} %share.1), channel_id=1, replica_groups=mesh['xh'=2,'xl'=2,'y'=4,'zab'=4,'zc'=2,'c'=2,'s'=4] {'s','zab'}, dimensions={0} | all-to-all | bytes 131072 | tf_op jit(solution)/shard_map/all_to_all | solution.py:285
  80.7 1.0 merge.1
  81.7 17.0 %all_to_all.29 = f32[32,8,768]{2,1,0:T(8,128)S(1)} all-to-all(f32[32,8,768]{2,1,0:T(8,128)S(1)} %bitcast.8), channel_id=1, replica_groups=mesh['xh'=2,'xl'=2,'y'=4,'zab'=4,'zc'=2,'c'=2,'s'=4] {'xh','xl','y','zc'}, dimensions={0} | all-to-all | bytes 1572864 | tf_op jit(solution)/shard_map/all_to_all | solution.py:285
  98.7 5.5 %collective-permute-start.1 = (f32[256,768]{1,0:T(8,128)S(1)}, f32[256,768]{1,0:T(8,128)S(1)}, u32[]{:S(2)}, u32[]{:S(2)}) collective-permute-start(f32[256,768]{1,0:T(8,128)S(1)} %bitcast.6), channel_id=1, source_target_pairs={{0,4},{4,0},{1,5},{5,1},{2,6},{6,2},{3,7},{7,3},{8,12},{12,8},{9,1... | collective-permute-start | bytes 2359304 | tf_op jit(solution)/shard_map/ppermute | solution.py:303
  104.9 1.2 %collective-permute-done.1.other_ref = f32[256,768]{1,0:T(8,128)S(1)} collective-permute-done((f32[256,768]{1,0:T(8,128)S(1)}, f32[256,768]{1,0:T(8,128)S(1)}, u32[]{:S(2)}, u32[]{:S(2)}) %collective-permute-start.1) | collective-permute-done | bytes 786464 | tf_op jit(solution)/shard_map/ppermute | solution.py:303
  106.1 0.0 copy-done.3
  106.1 2.1 %losses.1 = (f32[1,768]{1,0:T(1,128)}, f32[1,768]{1,0:T(1,128)}, f32[1,1]{1,0:T(1,128)}) custom-call(f32[1]{0:T(128)} %bitcast.5.scale_ref, s32[1,256]{1,0:T(1,128)S(1)} %bitcast.9, f32[256,768]{1,0:T(8,128)S(1)} %bitcast.7, f32[256,768]{1,0:T(8,128)S(1)} %collective-permute-done.1.other_ref), custom_call_target="tpu_custom_call" | custom-call | tf_op jit(solution)/shard_map/losses/pallas_call | solution.py:269
  (1 shorter events, 0.0 us)
Async XLA Ops:
  0.6 1.0 copy-start.4
  0.6 21.6 %copy-start = (bf16[1,512,3200]{2,1,0:T(8,128)(2,1)S(1)}, bf16[1,512,3200]{2,1,0:T(8,128)(2,1)}, u32[]{:S(2)}) copy-start(bf16[1,512,3200]{2,1,0:T(8,128)(2,1)} %tok_ref.1) | copy-start | bytes 9830404
  0.7 21.6 %copy-start.1 = (bf16[16,200]{1,0:T(8,128)(2,1)S(1)}, bf16[16,200]{1,0:T(8,128)(2,1)}, u32[]{:S(2)}) copy-start(bf16[16,200]{1,0:T(8,128)(2,1)} %query_ref.1) | copy-start | bytes 19204
  1.5 44.9 %copy-start.2 = (f32[1,768]{1,0:T(1,128)S(1)}, f32[1,768]{1,0:T(1,128)}, u32[]{:S(2)}) copy-start(f32[1,768]{1,0:T(1,128)} %text_ref.1) | copy-start | bytes 9220
  1.6 104.5 %copy-start.3 = (s32[256]{0:T(256)S(1)}, s32[256]{0:T(256)}, u32[]{:S(2)}) copy-start(s32[256]{0:T(256)} %param.12) | copy-start | bytes 3076
  1.6 35.0 %collective-permute-start = (bf16[200,768]{1,0:T(8,128)(2,1)S(1)}, bf16[200,768]{1,0:T(8,128)(2,1)S(1)}, u32[]{:S(2)}, u32[]{:S(2)}) collective-permute-start(bf16[200,768]{1,0:T(8,128)(2,1)S(1)} %copy-done.4), channel_id=1, source_target_pairs={{24,0},{51,8},{8,16},{32,24},{1,32},{16,40},{40,48},{56,56},{25,1}... | collective-permute-start | bytes 921608 | tf_op jit(solution)/shard_map/ppermute | solution.py:296
  98.7 7.4 %collective-permute-start.1 = (f32[256,768]{1,0:T(8,128)S(1)}, f32[256,768]{1,0:T(8,128)S(1)}, u32[]{:S(2)}, u32[]{:S(2)}) collective-permute-start(f32[256,768]{1,0:T(8,128)S(1)} %bitcast.6), channel_id=1, source_target_pairs={{0,4},{4,0},{1,5},{5,1},{2,6},{6,2},{3,7},{7,3},{8,12},{12,8},{9,1... | collective-permute-start | bytes 2359304 | tf_op jit(solution)/shard_map/ppermute | solution.py:303

commit v7 on v6

--- a/solution.py
+++ b/solution.py
@@ -186,7 +186,8 @@
 
 
 def merge_kernel(parts_ref, out_ref, video_ref, rows):
-    ends = [parts_ref[4 * s : 4 * (s + 1), 7, :] for s in range(4)]
+    own = [pl.ds(s, 4, stride=4) for s in range(4)]
+    ends = [parts_ref[own[s], 7, :] for s in range(4)]
     tops = [end[:, 64 : 64 + H] for end in ends]
     totals = [end[:, 80 : 80 + H] for end in ends]
     top = jnp.maximum(jnp.maximum(tops[0], tops[1]), jnp.maximum(tops[2], tops[3]))
@@ -201,9 +202,9 @@
     pooled = jnp.zeros((4, E), F32)
     texts = []
     for s in range(4):
-        mine = [parts_ref[4 * s : 4 * (s + 1), r, :] for r in range(6)]
+        mine = [parts_ref[own[s], r, :] for r in range(6)]
         pooled = pooled + factors[4 * s : 4 * (s + 1)] * jnp.concatenate(mine, axis=1)
-        texts += [parts_ref[4 * s : 4 * (s + 1), 6, :], ends[s][:, 0:64]]
+        texts += [parts_ref[own[s], 6, :], ends[s][:, 0:64]]
     videos = unit_rows(pooled)
     texts = unit_rows(jnp.concatenate(texts, axis=1))
     rows[0:4, :] = videos
@@ -225,13 +226,14 @@
 
 
 def clip_of(row):
-    return (row % 128 // 8) * 16 + (row % 4) * 4 + (row // 4 % 2) * 2 + row // 128
+    column = (row // 8 % 4) * 4 + row % 128 // 32
+    return column * 16 + (row % 4) * 4 + (row // 4 % 2) * 2 + row // 128
 
 
 def loss_kernel(scale_ref, pair_ref, mine_ref, other_ref, video_ref, text_ref, loss_ref, videos, texts, grads):
     core = lax.axis_index("c")
     here = lax.axis_index("xh") * 2 + lax.axis_index("xl")
-    place = ((here * 4 + lax.axis_index("y")) * 2 + lax.axis_index("zc")) * 4 + lax.axis_index("zab")
+    place = ((lax.axis_index("y") * 4 + here) * 2 + lax.axis_index("zc")) * 4 + lax.axis_index("zab")
     n = 256
     for ref, start in ((mine_ref, core * 128), (other_ref, (1 - core) * 128)):
         start = pl.multiple_of(start, 128)
@@ -297,9 +299,9 @@
     parts, state = pool(used, query, tokens)
     parts = exchange(parts, GROUP)
     sums = exchange(project(parts, weight), GROUP)
-    gathered = exchange(share(sums, state, text_feat), ("s", "zab"))
+    gathered = exchange(share(sums, state, text_feat), ("zab", "s"))
     block, video_embed = merge(gathered)
-    mine = exchange(block, ("xh", "xl", "y", "zc"))
+    mine = exchange(block, ("y", "xh", "xl", "zc"))
     other = lax.ppermute(mine, "c", [(0, 1), (1, 0)])
     grad_video, grad_text, loss = losses(logit_scale.reshape(1), pair.reshape(1, -1), mine, other)
     return (video_embed, grad_video, grad_text, loss.reshape(()))

time: 108 us -> 108 us (level)
  no operation moved by 1% of the time
where the time goes in v7:
time: 108 us
  blocking collectives  72.2 us (67%)
  starting transfers between devices  26.8 us (25%)
  Pallas kernels  5.56 us (5%)
  between operations  2.17 us (2%)
  waiting for transfers between devices  1.25 us (1%)
    all_to_all x4, blocking collectives, exchange(): return lax.all_to_all(value, axes, 0, 0, tiled=True)  72.2 us
    ppermute x1, starting transfers between devices, shards(): weight = lax.ppermute(value_weight, ('xl', 'y', 'zab', 'zc', 's'), moves)  20.7 us
    ppermute x1, starting transfers between devices, shards(): other = lax.ppermute(mine, 'c', [(0, 1), (1, 0)])  6.14 us
  transfers between devices with their start and end apart: 2, of which 1 were waited for; matrix products, arithmetic and copies ran while one was open for 0% of the time, Pallas kernels for 2%

profile of v7, /device:TPU:1, one launch (start us, length us, event | category | flops | bytes accessed | tf_op | source)
XLA Modules:
  0.0 108.1 jit_solution(11739162871363521108)
XLA Ops:
  0.6 0.0 copy-start.4
  0.6 0.0 copy-start
  0.7 0.0 copy-start.1
  1.5 0.0 copy-start.2
  1.5 0.1 copy-done.4
  1.6 0.0 copy-start.3
  1.6 20.7 %collective-permute-start = (bf16[200,768]{1,0:T(8,128)(2,1)S(1)}, bf16[200,768]{1,0:T(8,128)(2,1)S(1)}, u32[]{:S(2)}, u32[]{:S(2)}) collective-permute-start(bf16[200,768]{1,0:T(8,128)(2,1)S(1)} %copy-done.4), channel_id=1, source_target_pairs={{24,0},{51,8},{8,16},{32,24},{1,32},{16,40},{40,48},{56,56},{25,1}... | collective-permute-start | bytes 921608 | tf_op jit(solution)/shard_map/ppermute | solution.py:298
  22.3 0.0 copy-done
  22.3 0.0 copy-done.1
  22.3 1.8 %pool.1 = (f32[16,16,256]{2,1,0:T(8,128)S(1)}, f32[8,128]{1,0:T(8,128)S(1)}) custom-call(s32[8,128]{1,0:T(8,128)S(1)} %used_frames.1.used_ref, bf16[16,200]{1,0:T(8,128)(2,1)S(1)} %copy-done.1, bf16[1,512,3200]{2,1,0:T(8,128)(2,1)S(1)} %copy-done), custom_call_target="tpu_custom_call" | custom-call | flops 419430400 | bytes 3276800 | tf_op jit(solution)/shard_map/pool/pallas_call | solution.py:107
  24.1 12.4 %all_to_all.26.parts_ref = f32[16,16,256]{2,1,0:T(8,128)S(1)} all-to-all(f32[16,16,256]{2,1,0:T(8,128)S(1)} %get-tuple-element.14), channel_id=1, replica_groups=mesh['xh'=2,'xl'=2,'y'=4,'zab'=4,'zc'=2,'c'=2,'s'=4] {'xl','y','c'}, dimensions={0} | all-to-all | bytes 524288 | tf_op jit(solution)/shard_map/all_to_all | solution.py:287
  36.6 0.0 collective-permute-done.weight_ref
  36.6 0.5 project.1
  37.1 9.3 %all_to_all.27.sums_ref = f32[16,8,128]{2,1,0:T(8,128)S(1)} all-to-all(f32[16,8,128]{2,1,0:T(8,128)S(1)} %project.1), channel_id=1, replica_groups=mesh['xh'=2,'xl'=2,'y'=4,'zab'=4,'zc'=2,'c'=2,'s'=4] {'xl','y','c'}, dimensions={0} | all-to-all | bytes 131072 | tf_op jit(solution)/shard_map/all_to_all | solution.py:287
  46.4 0.0 copy-done.2
  46.4 0.1 share.1
  46.5 34.0 %all_to_all.28.parts_ref = f32[16,8,128]{2,1,0:T(8,128)S(1)} all-to-all(f32[16,8,128]{2,1,0:T(8,128)S(1)} %share.1), channel_id=1, replica_groups=mesh['xh'=2,'xl'=2,'y'=4,'zab'=4,'zc'=2,'c'=2,'s'=4] {'zab','s'}, dimensions={0} | all-to-all | bytes 131072 | tf_op jit(solution)/shard_map/all_to_all | solution.py:287
  80.5 1.0 merge.1
  81.5 16.4 %all_to_all.29 = f32[32,8,768]{2,1,0:T(8,128)S(1)} all-to-all(f32[32,8,768]{2,1,0:T(8,128)S(1)} %bitcast.8), channel_id=1, replica_groups=mesh['xh'=2,'xl'=2,'y'=4,'zab'=4,'zc'=2,'c'=2,'s'=4] {'y','xh','xl','zc'}, dimensions={0} | all-to-all | bytes 1572864 | tf_op jit(solution)/shard_map/all_to_all | solution.py:287
  98.0 6.1 %collective-permute-start.1 = (f32[256,768]{1,0:T(8,128)S(1)}, f32[256,768]{1,0:T(8,128)S(1)}, u32[]{:S(2)}, u32[]{:S(2)}) collective-permute-start(f32[256,768]{1,0:T(8,128)S(1)} %bitcast.6), channel_id=1, source_target_pairs={{0,4},{4,0},{1,5},{5,1},{2,6},{6,2},{3,7},{7,3},{8,12},{12,8},{9,1... | collective-permute-start | bytes 2359304 | tf_op jit(solution)/shard_map/ppermute | solution.py:305
  104.7 1.2 %collective-permute-done.1.other_ref = f32[256,768]{1,0:T(8,128)S(1)} collective-permute-done((f32[256,768]{1,0:T(8,128)S(1)}, f32[256,768]{1,0:T(8,128)S(1)}, u32[]{:S(2)}, u32[]{:S(2)}) %collective-permute-start.1) | collective-permute-done | bytes 786464 | tf_op jit(solution)/shard_map/ppermute | solution.py:305
  106.0 0.0 copy-done.3
  106.0 2.1 %losses.1 = (f32[1,768]{1,0:T(1,128)}, f32[1,768]{1,0:T(1,128)}, f32[1,1]{1,0:T(1,128)}) custom-call(f32[1]{0:T(128)} %bitcast.5.scale_ref, s32[1,256]{1,0:T(1,128)S(1)} %bitcast.9, f32[256,768]{1,0:T(8,128)S(1)} %bitcast.7, f32[256,768]{1,0:T(8,128)S(1)} %collective-permute-done.1.other_ref), custom_call_target="tpu_custom_call" | custom-call | tf_op jit(solution)/shard_map/losses/pallas_call | solution.py:271
  (1 shorter events, 0.0 us)
Async XLA Ops:
  0.6 1.0 copy-start.4
  0.6 21.6 %copy-start = (bf16[1,512,3200]{2,1,0:T(8,128)(2,1)S(1)}, bf16[1,512,3200]{2,1,0:T(8,128)(2,1)}, u32[]{:S(2)}) copy-start(bf16[1,512,3200]{2,1,0:T(8,128)(2,1)} %tok_ref.1) | copy-start | bytes 9830404
  0.7 21.6 %copy-start.1 = (bf16[16,200]{1,0:T(8,128)(2,1)S(1)}, bf16[16,200]{1,0:T(8,128)(2,1)}, u32[]{:S(2)}) copy-start(bf16[16,200]{1,0:T(8,128)(2,1)} %query_ref.1) | copy-start | bytes 19204
  1.5 44.9 %copy-start.2 = (f32[1,768]{1,0:T(1,128)S(1)}, f32[1,768]{1,0:T(1,128)}, u32[]{:S(2)}) copy-start(f32[1,768]{1,0:T(1,128)} %text_ref.1) | copy-start | bytes 9220
  1.6 104.4 %copy-start.3 = (s32[256]{0:T(256)S(1)}, s32[256]{0:T(256)}, u32[]{:S(2)}) copy-start(s32[256]{0:T(256)} %param.12) | copy-start | bytes 3076
  1.6 35.0 %collective-permute-start = (bf16[200,768]{1,0:T(8,128)(2,1)S(1)}, bf16[200,768]{1,0:T(8,128)(2,1)S(1)}, u32[]{:S(2)}, u32[]{:S(2)}) collective-permute-start(bf16[200,768]{1,0:T(8,128)(2,1)S(1)} %copy-done.4), channel_id=1, source_target_pairs={{24,0},{51,8},{8,16},{32,24},{1,32},{16,40},{40,48},{56,56},{25,1}... | collective-permute-start | bytes 921608 | tf_op jit(solution)/shard_map/ppermute | solution.py:298
  98.0 8.0 %collective-permute-start.1 = (f32[256,768]{1,0:T(8,128)S(1)}, f32[256,768]{1,0:T(8,128)S(1)}, u32[]{:S(2)}, u32[]{:S(2)}) collective-permute-start(f32[256,768]{1,0:T(8,128)S(1)} %bitcast.6), channel_id=1, source_target_pairs={{0,4},{4,0},{1,5},{5,1},{2,6},{6,2},{3,7},{7,3},{8,12},{12,8},{9,1... | collective-permute-start | bytes 2359304 | tf_op jit(solution)/shard_map/ppermute | solution.py:305

commit v8 on v7

--- a/solution.py
+++ b/solution.py
@@ -15,7 +15,7 @@
 HIGH = lax.Precision.HIGHEST
 F32, BF16 = jnp.float32, jnp.bfloat16
 VMEM_LIMIT = 40 * 1024 * 1024
-GROUP = ("xl", "y", "c")
+GROUP = ("c", "xl", "y")
 
 
 PAIRS = (
@@ -96,7 +96,7 @@
         members = jnp.where(zl == place, jnp.int32(code), members)
     for k in range(CHUNKS):
         member = (members >> (3 * (k // 2))) & 7
-        parts_ref[2 * member + k % 2, :, 0:ROWS] = mixed[:, ROWS * k : ROWS * (k + 1)]
+        parts_ref[8 * (k % 2) + member, :, 0:ROWS] = mixed[:, ROWS * k : ROWS * (k + 1)]
     lane = lax.broadcasted_iota(jnp.int32, (H, 128), 1)
     head = lax.broadcasted_iota(jnp.int32, (H, 128), 0)
     row = jnp.where(lane == 64 + head, top, 0.0) + jnp.where(lane == 80 + head, total, 0.0)

time: 108 us -> 108 us (level)
  no operation moved by 1% of the time
where the time goes in v8:
time: 108 us
  blocking collectives  71.8 us (66%)
  starting transfers between devices  26.9 us (25%)
  Pallas kernels  5.56 us (5%)
  between operations  2.17 us (2%)
  waiting for transfers between devices  1.25 us (1%)
    all_to_all x4, blocking collectives, exchange(): return lax.all_to_all(value, axes, 0, 0, tiled=True)  71.8 us
    ppermute x1, starting transfers between devices, shards(): weight = lax.ppermute(value_weight, ('xl', 'y', 'zab', 'zc', 's'), moves)  20.7 us
    ppermute x1, starting transfers between devices, shards(): other = lax.ppermute(mine, 'c', [(0, 1), (1, 0)])  6.18 us
  transfers between devices with their start and end apart: 2, of which 1 were waited for; matrix products, arithmetic and copies ran while one was open for 0% of the time, Pallas kernels for 2%

profile of v8, /device:TPU:1, one launch (start us, length us, event | category | flops | bytes accessed | tf_op | source)
XLA Modules:
  0.0 107.8 jit_solution(16491266039860334329)
XLA Ops:
  0.6 0.0 copy-start.4
  0.6 0.0 copy-start
  0.7 0.0 copy-start.1
  1.5 0.0 copy-start.2
  1.5 0.1 copy-done.4
  1.6 0.0 copy-start.3
  1.6 20.7 %collective-permute-start = (bf16[200,768]{1,0:T(8,128)(2,1)S(1)}, bf16[200,768]{1,0:T(8,128)(2,1)S(1)}, u32[]{:S(2)}, u32[]{:S(2)}) collective-permute-start(bf16[200,768]{1,0:T(8,128)(2,1)S(1)} %copy-done.4), channel_id=1, source_target_pairs={{24,0},{51,8},{8,16},{32,24},{1,32},{16,40},{40,48},{56,56},{25,1}... | collective-permute-start | bytes 921608 | tf_op jit(solution)/shard_map/ppermute | solution.py:298
  22.3 0.0 copy-done
  22.3 0.0 copy-done.1
  22.3 1.8 %pool.1 = (f32[16,16,256]{2,1,0:T(8,128)S(1)}, f32[8,128]{1,0:T(8,128)S(1)}) custom-call(s32[8,128]{1,0:T(8,128)S(1)} %used_frames.1.used_ref, bf16[16,200]{1,0:T(8,128)(2,1)S(1)} %copy-done.1, bf16[1,512,3200]{2,1,0:T(8,128)(2,1)S(1)} %copy-done), custom_call_target="tpu_custom_call" | custom-call | flops 419430400 | bytes 3276800 | tf_op jit(solution)/shard_map/pool/pallas_call | solution.py:107
  24.1 13.0 %all_to_all.26.parts_ref = f32[16,16,256]{2,1,0:T(8,128)S(1)} all-to-all(f32[16,16,256]{2,1,0:T(8,128)S(1)} %get-tuple-element.14), channel_id=1, replica_groups=mesh['xh'=2,'xl'=2,'y'=4,'zab'=4,'zc'=2,'c'=2,'s'=4] {'c','xl','y'}, dimensions={0} | all-to-all | bytes 524288 | tf_op jit(solution)/shard_map/all_to_all | solution.py:287
  37.2 0.0 collective-permute-done.weight_ref
  37.2 0.5 project.1
  37.7 8.8 %all_to_all.27.sums_ref = f32[16,8,128]{2,1,0:T(8,128)S(1)} all-to-all(f32[16,8,128]{2,1,0:T(8,128)S(1)} %project.1), channel_id=1, replica_groups=mesh['xh'=2,'xl'=2,'y'=4,'zab'=4,'zc'=2,'c'=2,'s'=4] {'c','xl','y'}, dimensions={0} | all-to-all | bytes 131072 | tf_op jit(solution)/shard_map/all_to_all | solution.py:287
  46.5 0.0 copy-done.2
  46.5 0.1 share.1
  46.6 34.0 %all_to_all.28.parts_ref = f32[16,8,128]{2,1,0:T(8,128)S(1)} all-to-all(f32[16,8,128]{2,1,0:T(8,128)S(1)} %share.1), channel_id=1, replica_groups=mesh['xh'=2,'xl'=2,'y'=4,'zab'=4,'zc'=2,'c'=2,'s'=4] {'zab','s'}, dimensions={0} | all-to-all | bytes 131072 | tf_op jit(solution)/shard_map/all_to_all | solution.py:287
  80.6 1.0 merge.1
  81.6 16.0 %all_to_all.29 = f32[32,8,768]{2,1,0:T(8,128)S(1)} all-to-all(f32[32,8,768]{2,1,0:T(8,128)S(1)} %bitcast.8), channel_id=1, replica_groups=mesh['xh'=2,'xl'=2,'y'=4,'zab'=4,'zc'=2,'c'=2,'s'=4] {'y','xh','xl','zc'}, dimensions={0} | all-to-all | bytes 1572864 | tf_op jit(solution)/shard_map/all_to_all | solution.py:287
  97.6 6.2 %collective-permute-start.1 = (f32[256,768]{1,0:T(8,128)S(1)}, f32[256,768]{1,0:T(8,128)S(1)}, u32[]{:S(2)}, u32[]{:S(2)}) collective-permute-start(f32[256,768]{1,0:T(8,128)S(1)} %bitcast.6), channel_id=1, source_target_pairs={{0,4},{4,0},{1,5},{5,1},{2,6},{6,2},{3,7},{7,3},{8,12},{12,8},{9,1... | collective-permute-start | bytes 2359304 | tf_op jit(solution)/shard_map/ppermute | solution.py:305
  104.4 1.2 %collective-permute-done.1.other_ref = f32[256,768]{1,0:T(8,128)S(1)} collective-permute-done((f32[256,768]{1,0:T(8,128)S(1)}, f32[256,768]{1,0:T(8,128)S(1)}, u32[]{:S(2)}, u32[]{:S(2)}) %collective-permute-start.1) | collective-permute-done | bytes 786464 | tf_op jit(solution)/shard_map/ppermute | solution.py:305
  105.7 0.0 copy-done.3
  105.7 2.1 %losses.1 = (f32[1,768]{1,0:T(1,128)}, f32[1,768]{1,0:T(1,128)}, f32[1,1]{1,0:T(1,128)}) custom-call(f32[1]{0:T(128)} %bitcast.5.scale_ref, s32[1,256]{1,0:T(1,128)S(1)} %bitcast.9, f32[256,768]{1,0:T(8,128)S(1)} %bitcast.7, f32[256,768]{1,0:T(8,128)S(1)} %collective-permute-done.1.other_ref), custom_call_target="tpu_custom_call" | custom-call | tf_op jit(solution)/shard_map/losses/pallas_call | solution.py:271
  (1 shorter events, 0.0 us)
Async XLA Ops:
  0.6 1.0 copy-start.4
  0.6 21.6 %copy-start = (bf16[1,512,3200]{2,1,0:T(8,128)(2,1)S(1)}, bf16[1,512,3200]{2,1,0:T(8,128)(2,1)}, u32[]{:S(2)}) copy-start(bf16[1,512,3200]{2,1,0:T(8,128)(2,1)} %tok_ref.1) | copy-start | bytes 9830404
  0.7 21.6 %copy-start.1 = (bf16[16,200]{1,0:T(8,128)(2,1)S(1)}, bf16[16,200]{1,0:T(8,128)(2,1)}, u32[]{:S(2)}) copy-start(bf16[16,200]{1,0:T(8,128)(2,1)} %query_ref.1) | copy-start | bytes 19204
  1.5 45.0 %copy-start.2 = (f32[1,768]{1,0:T(1,128)S(1)}, f32[1,768]{1,0:T(1,128)}, u32[]{:S(2)}) copy-start(f32[1,768]{1,0:T(1,128)} %text_ref.1) | copy-start | bytes 9220
  1.6 104.1 %copy-start.3 = (s32[256]{0:T(256)S(1)}, s32[256]{0:T(256)}, u32[]{:S(2)}) copy-start(s32[256]{0:T(256)} %param.12) | copy-start | bytes 3076
  1.6 35.6 %collective-permute-start = (bf16[200,768]{1,0:T(8,128)(2,1)S(1)}, bf16[200,768]{1,0:T(8,128)(2,1)S(1)}, u32[]{:S(2)}, u32[]{:S(2)}) collective-permute-start(bf16[200,768]{1,0:T(8,128)(2,1)S(1)} %copy-done.4), channel_id=1, source_target_pairs={{24,0},{51,8},{8,16},{32,24},{1,32},{16,40},{40,48},{56,56},{25,1}... | collective-permute-start | bytes 921608 | tf_op jit(solution)/shard_map/ppermute | solution.py:298
  97.6 8.1 %collective-permute-start.1 = (f32[256,768]{1,0:T(8,128)S(1)}, f32[256,768]{1,0:T(8,128)S(1)}, u32[]{:S(2)}, u32[]{:S(2)}) collective-permute-start(f32[256,768]{1,0:T(8,128)S(1)} %bitcast.6), channel_id=1, source_target_pairs={{0,4},{4,0},{1,5},{5,1},{2,6},{6,2},{3,7},{7,3},{8,12},{12,8},{9,1... | collective-permute-start | bytes 2359304 | tf_op jit(solution)/shard_map/ppermute | solution.py:305
